TPU v7x, 512 devices: a whole 4x4x16 slice. The times are simulated.
512 devices in a mesh: row: 16 (over y, x), col: 32 (over z, core).
Axes of the slice: x: 4, y: 4, z: 16, core: 2. Of those that a mesh axis runs over, the one named last changes fastest.
Arguments:
- hidden: bfloat16 [512, 16384], P('col', 'row'), may hold values from -6 to 6
- cotangent: bfloat16 [512, 16384], P('col', 'row'), may hold values from -6 to 6
- importance: bfloat16 [512], P('col'), may hold values from 0.099609375 to 10
- positions: int32 [512], P('col'), may hold values from 0 to 4606, as said below
- segments: int32 [512], P('col'), may hold values from 0 to 3, as said below
- norm_gain: bfloat16 [16384], P('row'), may hold values from 0.5 to 1.5
- query_weight_matrix: bfloat16 [16384, 16384], P('row', 'col')
- key_weight: bfloat16 [16384, 1024], P('row', 'col')
- value_weight_matrix: bfloat16 [16384, 1024], P('row', 'col'), may hold values from -0.046875 to 0.046875
- output_weight_matrix: bfloat16 [16384, 16384], P('col', 'row'), may hold values from -0.046875 to 0.046875
- query_down_factor: bfloat16 [16384, 64], P('row'), may hold values from -0.046875 to 0.046875
- query_up_factor: bfloat16 [64, 16384], P(None, 'col'), may hold values from -0.75 to 0.75
- output_down_factor: bfloat16 [16384, 64], P('col'), may hold values from -0.046875 to 0.046875
- out_up: bfloat16 [64, 16384], P(None, 'row'), may hold values from -0.75 to 0.75
Outputs:
- input_grad: float32 [512, 16384], P('col', 'row')
- query_down_gradient: float32 [16384, 64], P('row')
- query_up_gradient: float32 [64, 16384], P(None, 'col')
- output_down_gradient: float32 [16384, 64], P('col')
- output_up_gradient: float32 [64, 16384], P(None, 'row')
Inputs may be any that keep to these rules, and one draw needn't show every extreme that they name: `segments`: rollout numbers never fall along the tokens, and each of the 4 rollouts holds at least one token. positions rise by one from token to token within a rollout.
All inputs are finite; a program needn't handle non-finite values.
Results may differ from a plain program's by a relative error of at most 0.012.
The roundings to bfloat16 on the way count: a program that leaves them out, or rounds other values in their place, can miss the bound.
Values may be sent and summed in bfloat16 or wider, within the bound.
A program may use at most 64 MiB of HBM per device.

v0:
```python
import math

import jax
import jax.numpy as jnp
from jax import lax
from jax.sharding import PartitionSpec as P

MODEL_WIDTH = 16384
KEY_VALUE_HEADS = 8
HEAD_SIZE = 128


norm_eps = 1e-05
adapter_scale = 2.0
ratio_cap = 2.0
rope_base = 500000.0
masked_fill = -1e30


def from_partner(block, axis, bit):
    count = lax.axis_size(axis)
    route = []
    for low in range(count):
        high = low | 1 << bit
        if high != low and high < count:
            route += [(low, high), (high, low)]
    return lax.ppermute(block, axis, route)


def narrow_precision(tensor):
    return lax.optimization_barrier(tensor.astype(jnp.bfloat16))


def matrix_product(left, right):
    return jnp.dot(left, right, preferred_element_type=jnp.float32)


def rope_tables(position_ids, head_width):
    half_width = head_width // 2
    frequency = jnp.exp(
        jnp.arange(half_width, dtype=jnp.float32) * (-2.0 * math.log(rope_base) / head_width)
    )
    angles = position_ids.astype(jnp.float32)[:, None] * frequency[None, :]
    return (jnp.cos(angles)[:, None, :], jnp.sin(angles)[:, None, :])


def apply_rotation(tensor, cosine_lookup, sine_lookup):
    half_width = tensor.shape[-1] // 2
    first_half = tensor[..., :half_width]
    second_half = tensor[..., half_width:]
    return jnp.concatenate(
        [
            first_half * cosine_lookup - second_half * sine_lookup,
            second_half * cosine_lookup + first_half * sine_lookup,
        ],
        axis=-1,
    )


def reverse_rotation(tensor, cosine_lookup, sine_lookup):
    half_width = tensor.shape[-1] // 2
    first_half = tensor[..., :half_width]
    second_half = tensor[..., half_width:]
    return jnp.concatenate(
        [
            first_half * cosine_lookup + second_half * sine_lookup,
            second_half * cosine_lookup - first_half * sine_lookup,
        ],
        axis=-1,
    )


def per_device(
    hidden,
    cotangent,
    importance,
    positions,
    segments,
    norm_gain,
    query_weight_matrix,
    key_weight,
    value_weight_matrix,
    output_weight_matrix,
    query_down_factor,
    query_up_factor,
    output_down_factor,
    out_up,
):
    column_total = lax.axis_size("col")
    col_place = lax.axis_index("col")
    own_tokens = hidden.shape[0]
    heads_here = query_weight_matrix.shape[1] // HEAD_SIZE
    group_members = column_total // KEY_VALUE_HEADS
    score_scale = HEAD_SIZE ** (-0.5)
    gain_wide = norm_gain.astype(jnp.float32)
    hidden_wide = hidden.astype(jnp.float32)
    weighted_own = narrow_precision(
        cotangent.astype(jnp.float32)
        * jnp.minimum(importance.astype(jnp.float32), ratio_cap)[:, None]
    )
    key_cols = key_weight
    value_cols = value_weight_matrix
    for bit_number in range(group_members.bit_length() - 1):
        other_key, other_value = from_partner((key_cols, value_cols), "col", bit_number)
        lower_side = col_place // (1 << bit_number) % 2 == 0
        key_cols = jnp.where(
            lower_side,
            jnp.concatenate([key_cols, other_key], axis=1),
            jnp.concatenate([other_key, key_cols], axis=1),
        )
        value_cols = jnp.where(
            lower_side,
            jnp.concatenate([value_cols, other_value], axis=1),
            jnp.concatenate([other_value, value_cols], axis=1),
        )
    hidden_all, weighted_all, position_all, segment_all = (
        lax.all_gather(hidden, "col", axis=0, tiled=True),
        lax.all_gather(weighted_own, "col", axis=0, tiled=True),
        lax.all_gather(positions, "col", axis=0, tiled=True),
        lax.all_gather(segments, "col", axis=0, tiled=True),
    )
    token_total = hidden_all.shape[0]
    hidden_all_wide = hidden_all.astype(jnp.float32)
    square_sum = lax.psum(jnp.sum(hidden_all_wide * hidden_all_wide, axis=1), "row")
    inverse_rms = lax.rsqrt(square_sum / MODEL_WIDTH + norm_eps)
    normalized = (hidden_all_wide * inverse_rms[:, None] * gain_wide[None, :]).astype(jnp.bfloat16)
    low_part = matrix_product(normalized, query_down_factor)
    key_part = matrix_product(normalized, key_cols)
    value_part = matrix_product(normalized, value_cols)
    query_total_sum, low_sum, key_sum, value_sum = lax.psum(
        (matrix_product(normalized, query_weight_matrix), low_part, key_part, value_part), "row"
    )
    reduced_query = low_sum.astype(jnp.bfloat16)
    query_linear_part = query_total_sum + adapter_scale * matrix_product(
        reduced_query, query_up_factor
    )
    query_cosine, query_sine = rope_tables(position_all, HEAD_SIZE)
    key_cosine, key_sine = rope_tables(position_all, HEAD_SIZE)
    queries = apply_rotation(
        query_linear_part.reshape(token_total, heads_here, HEAD_SIZE), query_cosine, query_sine
    ).astype(jnp.bfloat16)
    key_row_block = (
        apply_rotation(key_sum.reshape(token_total, 1, HEAD_SIZE), key_cosine, key_sine)
        .reshape(token_total, HEAD_SIZE)
        .astype(jnp.bfloat16)
    )
    value_row_block = value_sum.astype(jnp.bfloat16)
    query_index = jnp.arange(token_total, dtype=jnp.int32)
    key_index = jnp.arange(token_total, dtype=jnp.int32)
    allowed = (segment_all[:, None] == segment_all[None, :]) & (
        key_index[None, :] <= query_index[:, None]
    )
    scores = (
        jnp.einsum("qhd,kd->hqk", queries, key_row_block, preferred_element_type=jnp.float32)
        * score_scale
    )
    scores = jnp.where(allowed[None], scores, masked_fill)
    shifted = jnp.exp(scores - jnp.max(scores, axis=2, keepdims=True))
    attention_probs = shifted / jnp.sum(shifted, axis=2, keepdims=True)
    probs_narrow = attention_probs.astype(jnp.bfloat16)
    attended_rows = (
        jnp.einsum("hqk,kd->qhd", probs_narrow, value_row_block, preferred_element_type=jnp.float32)
        .astype(jnp.bfloat16)
        .reshape(token_total, heads_here * HEAD_SIZE)
    )
    low_grad_part = jnp.einsum(
        "td,rd->tr", weighted_all, out_up, preferred_element_type=jnp.float32
    )
    full_grad = jnp.einsum(
        "td,qd->tq", weighted_all, output_weight_matrix, preferred_element_type=jnp.float32
    )
    grad_rows, low_grad_sum = lax.psum((full_grad, low_grad_part), "row")
    low_out_part = jnp.einsum(
        "tq,qr->tr", attended_rows, output_down_factor, preferred_element_type=jnp.float32
    )
    low_out_sum = lax.psum(low_out_part, "col")
    reduced_gradient = low_grad_sum.astype(jnp.bfloat16)
    attention_grad = (
        grad_rows
        + adapter_scale
        * jnp.einsum(
            "tr,qr->tq", reduced_gradient, output_down_factor, preferred_element_type=jnp.float32
        )
    ).astype(jnp.bfloat16)
    output_down_gradient = adapter_scale * jnp.einsum(
        "tq,tr->qr", attended_rows, reduced_gradient, preferred_element_type=jnp.float32
    )
    head_grads = attention_grad.reshape(token_total, heads_here, HEAD_SIZE)
    prob_grad = jnp.einsum(
        "qhd,kd->hqk", head_grads, value_row_block, preferred_element_type=jnp.float32
    )
    row_dot = jnp.sum(attention_probs * prob_grad, axis=2, keepdims=True)
    score_grad = (attention_probs * (prob_grad - row_dot) * score_scale).astype(jnp.bfloat16)
    query_gradient_rotated = jnp.einsum(
        "hqk,kd->qhd", score_grad, key_row_block, preferred_element_type=jnp.float32
    )
    key_gradient = jnp.einsum(
        "hqk,qhd->kd", score_grad, queries, preferred_element_type=jnp.float32
    )
    value_gradient = jnp.einsum(
        "hqk,qhd->kd", probs_narrow, head_grads, preferred_element_type=jnp.float32
    )
    query_grad_rows = (
        reverse_rotation(query_gradient_rotated, query_cosine, query_sine)
        .reshape(token_total, heads_here * HEAD_SIZE)
        .astype(jnp.bfloat16)
    )
    key_grad_linear = reverse_rotation(
        key_gradient.reshape(token_total, 1, HEAD_SIZE), key_cosine, key_sine
    ).reshape(token_total, HEAD_SIZE)
    query_up_gradient = adapter_scale * jnp.einsum(
        "tr,tq->rq", reduced_query, query_grad_rows, preferred_element_type=jnp.float32
    )
    low_back_part = jnp.einsum(
        "tq,rq->tr", query_grad_rows, query_up_factor, preferred_element_type=jnp.float32
    )
    key_cols_wide = key_cols.astype(jnp.float32)
    value_cols_wide = value_cols.astype(jnp.float32)
    grad_block = jnp.einsum(
        "tq,dq->td", query_grad_rows, query_weight_matrix, preferred_element_type=jnp.float32
    )
    grad_block = grad_block + jnp.dot(
        key_grad_linear, key_cols_wide.T, precision=lax.Precision.HIGHEST
    )
    grad_block = grad_block + jnp.dot(
        value_gradient, value_cols_wide.T, precision=lax.Precision.HIGHEST
    )
    normalized_gradient = lax.psum_scatter(grad_block, "col", scatter_dimension=0, tiled=True)
    low_back_sum = lax.psum(low_back_part, "col")
    reduced_output = low_out_sum.astype(jnp.bfloat16)
    reduced_backprop = low_back_sum.astype(jnp.bfloat16)
    output_up_gradient = adapter_scale * jnp.einsum(
        "tr,td->rd", reduced_output, weighted_all, preferred_element_type=jnp.float32
    )
    query_down_gradient = adapter_scale * jnp.einsum(
        "td,tr->dr", normalized, reduced_backprop, preferred_element_type=jnp.float32
    )
    own_first = col_place * own_tokens
    low_back_own = lax.dynamic_slice_in_dim(reduced_backprop, own_first, own_tokens, 0)
    normalized_gradient = normalized_gradient + adapter_scale * jnp.einsum(
        "tr,dr->td", low_back_own, query_down_factor, preferred_element_type=jnp.float32
    )
    own_rms = lax.dynamic_slice_in_dim(inverse_rms, own_first, own_tokens, 0)
    dot_sum = lax.psum(
        jnp.sum(hidden_wide * gain_wide[None, :] * normalized_gradient, axis=1), "row"
    )
    input_grad = (
        weighted_own.astype(jnp.float32)
        + own_rms[:, None] * gain_wide[None, :] * normalized_gradient
        - hidden_wide * (own_rms**3 * dot_sum / MODEL_WIDTH)[:, None]
    )
    return (
        input_grad,
        query_down_gradient,
        query_up_gradient,
        output_down_gradient,
        output_up_gradient,
    )


def solution(mesh):
    placed = (
        P("col", "row"),
        P("col", "row"),
        P("col"),
        P("col"),
        P("col"),
        P("row"),
        P("row", "col"),
        P("row", "col"),
        P("row", "col"),
        P("col", "row"),
        P("row", None),
        P(None, "col"),
        P("col", None),
        P(None, "row"),
    )
    return jax.shard_map(
        per_device,
        mesh=mesh,
        in_specs=placed,
        out_specs=(P("col", "row"), P("row", None), P(None, "col"), P("col", None), P(None, "row")),
        check_vma=False,
    )
```

profile of v0, /device:TPU:1, one launch (start us, length us, event | category | flops | bytes accessed | tf_op | source)
XLA Modules:
  0.0 477.0 jit_solution(11623572333262443432)
XLA Ops:
  10.1 8.8 %collective-permute-start = (bf16[1024,32]{0,1:T(8,128)(2,1)}, bf16[1024,32]{0,1:T(8,128)(2,1)S(1)}, u32[]{:S(2)}, u32[]{:S(2)}) collective-permute-start(bf16[1024,32]{0,1:T(8,128)(2,1)} %param.21), channel_id=1, source_target_pairs={{0,1},{1,0},{2,3},{3,2},{4,5},{5,4},{6,7},{7,6},{8,9},{9,8},{10,11... | collective-permute-start | bytes 196616 | tf_op jit(solution)/shard_map/ppermute | solution.py:27
  21.0 1.9 collective-permute-start.1
  22.9 63.6 %all-gather.3.cloned.1.call-done = bf16[512,1024]{1,0:T(8,128)(2,1)} async-done(((bf16[16,1024]{1,0:T(8,128)(2,1)}), bf16[512,1024]{1,0:T(8,128)(2,1)}) %all-gather.3.cloned.1.call-update) | async-done | bytes 1048592 | tf_op jit(solution)/shard_map/all_gather | solution.py:117
  88.1 33.3 %psum.70 = f32[512]{0:T(512)S(1)} all-reduce(f32[512]{0:T(512)S(1)} %fusion.6), channel_id=1, replica_groups=mesh['row'=16,'col'=32] {'row'}, use_global_device_ids=true, to_apply=%region_1.2 | all-reduce | flops 512 | bytes 4096 | tf_op jit(solution)/shard_map/psum | solution.py:124
  121.4 2.5 convolution_bitcast_fusion.1
  123.9 1.8 fusion.80
  125.7 30.8 %all-gather.5.cloned.1.call-done = bf16[512,1024]{1,0:T(8,128)(2,1)} async-done(((bf16[16,1024]{1,0:T(8,128)(2,1)}), bf16[512,1024]{1,0:T(8,128)(2,1)}) %all-gather.5.cloned.1.call-update) | async-done | bytes 1048592 | tf_op jit(solution)/shard_map/all_gather | solution.py:118
  156.5 3.3 fusion.85
  159.9 2.2 collective-permute-start.2
  164.5 16.5 %all-reduce.2 = (s32[512]{0:T(512)S(1)}, s32[512]{0:T(512)S(1)}) all-reduce(s32[512]{0:T(512)S(1)} %dynamic-update-slice, s32[512]{0:T(512)S(1)} %dynamic-update-slice.1), channel_id=1, replica_groups=mesh['row'=16,'col'=32] {'col'}, use_global_device_ids=true, to_apply=%add | all-reduce | flops 1024 | bytes 8192
  181.1 1.8 multiply_cosine_fusion
  184.8 2.2 collective-permute-start.3
  187.0 2.0 fusion.86
  189.0 2.1 fusion.78
  192.9 68.1 %all-reduce.11 = (bf16[512,64]{0,1:T(8,128)(2,1)}, bf16[512,128]{1,0:T(8,128)(2,1)}, bf16[512,64]{0,1:T(8,128)(2,1)S(1)}) all-reduce(f32[512,64]{0,1:T(8,128)} %fusion.86, f32[512,128]{1,0:T(8,128)} %fusion.56, f32[512,64]{0,1:T(8,128)} %fusion.78), channel_id=1, replica_groups=mesh['row'=16,'col'=32] {'row'}, use_global_device_ids=true, to_apply=%region_9.10 | all-reduce | flops 131072 | bytes 786432 | tf_op jit(solution)/shard_map/psum | solution.py:172
  261.0 19.0 %all-reduce.10.cloned.1.call-done = (f32[512,512]{1,0:T(8,128)}, f32[512,1,128]{2,0,1:T(8,128)}, f32[512,512]{1,0:T(8,128)}) async-done(((f32[512,512]{1,0:T(8,128)}, f32[512,1,128]{2,0,1:T(8,128)}, f32[512,512]{1,0:T(8,128)}), (f32[512,512]{1,0:T(8,128)}, f32[512,1,128]{2,0,1:T(8,128)}, f32[512,512]{1,0:T(8,128)})) %all-reduce.10.cloned.1.call-update) | async-done | bytes 2359312 | tf_op jit(solution)/shard_map/psum | solution.py:172
  279.9 2.8 fusion.40
  282.8 2.5 fusion.17
  288.4 2.7 fusion.25
  292.2 5.7 %fusion.84 = (f32[4,512]{1,0:T(4,128)}, f32[4,512,512]{1,2,0:T(8,128)}) fusion(pred[512,512]{0,1:T(8,128)(4,1)} %fusion.23, bf16[512,1,64]{2,0,1:T(8,128)(2,1)} %get-tuple-element.26, bf16[512,1,64]{2,0,1:T(8,128)(2,1)} %get-tuple-element.25, bf16[512,4,64]{2,0,1:T(8,128)(2,1)} %get-tuple-element.18, bf16[512,4,64]{2,0,1:T(8,128)(2,1)S(1)} %get-tuple-element.17), kind=kOutput, calls=%fused_computation.120 | convolution fusion | flops 273940992 | bytes 5120000 | tf_op jit(solution)/shard_map/sub | solution.py:158
  297.9 3.6 convolution_bitcast_fusion
  301.5 8.5 %fusion.20 = f32[512,1,128]{2,0,1:T(8,128)} fusion(f32[512,512,4]{1,0,2:T(8,128)} %fusion.25, bf16[512,4,64]{2,0,1:T(8,128)(2,1)} %get-tuple-element.18, bf16[512,4,64]{2,0,1:T(8,128)(2,1)S(1)} %get-tuple-element.17, f32[4,512,512]{1,2,0:T(8,128)} %get-tuple-element.30, f32[4,512]{1,0:T(4,128)} %get-tuple-element.29), kind=kOutput, calls=%fused_computation.31 | convolution fusion | flops 276826624 | bytes 9183232 | tf_op jit(solution)/shard_map/hqk,qhd->kd/dot_general | solution.py:197
  310.0 7.8 %fusion.15 = f32[512,4,128]{2,0,1:T(8,128)S(1)} fusion(f32[512,512,4]{1,0,2:T(8,128)} %fusion.25, bf16[512,1,64]{2,0,1:T(8,128)(2,1)} %get-tuple-element.26, bf16[512,1,64]{2,0,1:T(8,128)(2,1)} %get-tuple-element.25, f32[4,512,512]{1,2,0:T(8,128)} %get-tuple-element.30, f32[4,512]{1,0:T(4,128)} %get-tuple-element.29), kind=kOutput, calls=%fused_computation.23 | convolution fusion | flops 276040192 | bytes 9576448 | tf_op jit(solution)/shard_map/hqk,kd->qhd/dot_general | solution.py:194
  319.8 2.4 fusion.43
  324.1 2.6 add_add_fusion
  326.8 2.7 convolution_convert_fusion
  330.1 94.2 %all-reduce.12 = (bf16[512,64]{0,1:T(8,128)(2,1)}, bf16[512,64]{1,0:T(8,128)(2,1)}) all-reduce(f32[512,64]{0,1:T(8,128)S(1)} %fusion.89, f32[512,64]{1,0:T(8,128)S(1)} %fusion.88), channel_id=1, replica_groups=mesh['row'=16,'col'=32] {'col'}, use_global_device_ids=true, to_apply=%region_12.13 | all-reduce | flops 65536 | bytes 393216 | tf_op jit(solution)/shard_map/psum | solution.py:229
  424.3 1.8 convolution_multiply_fusion.4
  426.1 1.8 convolution_multiply_fusion.5
  427.9 2.4 convolution_multiply_fusion.2
  430.3 1.9 convolution_multiply_fusion.3
  435.0 33.8 %psum.78 = f32[16]{0:T(128)S(1)} all-reduce(f32[16]{0:T(128)S(1)} %get-tuple-element.31), channel_id=1, replica_groups=mesh['row'=16,'col'=32] {'row'}, use_global_device_ids=true, to_apply=%region_14.15 | all-reduce | flops 16 | bytes 128 | tf_op jit(solution)/shard_map/psum | solution.py:244
  (99 shorter events, 24.9 us)
Async XLA Ops:
  7.2 116.7 %copy-start = (bf16[1024,512]{1,0:T(8,128)(2,1)S(1)}, bf16[1024,512]{1,0:T(8,128)(2,1)}, u32[]{:S(2)}) copy-start(bf16[1024,512]{1,0:T(8,128)(2,1)} %param.20) | copy-start | bytes 3145732
  7.2 79.4 %all-gather.3.cloned.1.call-start = ((), (), s32[]{:S(2)}) async-start(), calls=%async_computation.1 | async-start | bytes 1081344 | tf_op jit(solution)/shard_map/all_gather | solution.py:117
  7.9 148.6 %all-gather.5.cloned.1.call-start = ((), (), s32[]{:S(2)}) async-start(), calls=%async_computation.2 | async-start | bytes 1081344 | tf_op jit(solution)/shard_map/all_gather | solution.py:118
  10.1 269.9 %all-reduce.10.cloned.1.call-start = ((), (), s32[]{:S(2)}) async-start(), calls=%async_computation.4 | async-start | bytes 4718592 | tf_op jit(solution)/shard_map/psum | solution.py:172
  10.1 9.9 %collective-permute-start = (bf16[1024,32]{0,1:T(8,128)(2,1)}, bf16[1024,32]{0,1:T(8,128)(2,1)S(1)}, u32[]{:S(2)}, u32[]{:S(2)}) collective-permute-start(bf16[1024,32]{0,1:T(8,128)(2,1)} %param.21), channel_id=1, source_target_pairs={{0,1},{1,0},{2,3},{3,2},{4,5},{5,4},{6,7},{7,6},{8,9},{9,8},{10,11... | collective-permute-start | bytes 196616 | tf_op jit(solution)/shard_map/ppermute | solution.py:27
  21.0 100.4 %collective-permute-start.1 = (bf16[1024,64]{0,1:T(8,128)(2,1)S(1)}, bf16[1024,64]{0,1:T(8,128)(2,1)S(1)}, u32[]{:S(2)}, u32[]{:S(2)}) collective-permute-start(bf16[1024,64]{0,1:T(8,128)(2,1)S(1)} %maximum_select_fusion.2), channel_id=1, source_target_pairs={{0,2},{2,0},{1,3},{3,1},{4,6},{6,4},{5,7},{7,5},{8,10},{10,8},{9,1... | collective-permute-start | bytes 393224 | tf_op jit(solution)/shard_map/ppermute | solution.py:27
  86.5 37.3 %copy-start.3 = (bf16[512,1024]{1,0:T(8,128)(2,1)S(1)}, bf16[512,1024]{1,0:T(8,128)(2,1)}, u32[]{:S(2)}) copy-start(bf16[512,1024]{1,0:T(8,128)(2,1)} %all-gather.3.cloned.1.call-done) | copy-start | bytes 3145732
  121.4 38.4 %copy-start.22 = (f32[512]{0:T(512)}, f32[512]{0:T(512)S(1)}, u32[]{:S(2)}) copy-start(f32[512]{0:T(512)S(1)} %add_rsqrt_fusion) | copy-start | bytes 6148
  121.4 38.4 %copy-start.15 = (bf16[1024,64]{0,1:T(8,128)(2,1)}, bf16[1024,64]{0,1:T(8,128)(2,1)S(1)}, u32[]{:S(2)}) copy-start(bf16[1024,64]{0,1:T(8,128)(2,1)S(1)} %collective-permute-done.1) | copy-start | bytes 393220
  123.9 40.2 %copy-start.25 = (s32[16]{0:T(128)S(1)}, s32[16]{0:T(128)}, u32[]{:S(2)}) copy-start(s32[16]{0:T(128)} %param.17) | copy-start | bytes 196
  123.9 40.4 %copy-start.26 = (s32[16]{0:T(128)S(1)}, s32[16]{0:T(128)}, u32[]{:S(2)}) copy-start(s32[16]{0:T(128)} %param.18) | copy-start | bytes 196
  156.5 30.5 %copy-start.1 = (bf16[512,1024]{1,0:T(8,128)(2,1)S(1)}, bf16[512,1024]{1,0:T(8,128)(2,1)}, u32[]{:S(2)}) copy-start(bf16[512,1024]{1,0:T(8,128)(2,1)} %all-gather.5.cloned.1.call-done) | copy-start | bytes 3145732
  159.9 273.9 %reduce-scatter.2.cloned.1.call-start = ((), (), s32[]{:S(2)}) async-start(), calls=%async_computation.3 | async-start | bytes 2162688 | tf_op jit(solution)/shard_map/reduce_scatter | solution.py:228
  159.9 23.9 %collective-permute-start.2 = (bf16[1024,32]{0,1:T(8,128)(2,1)}, bf16[1024,32]{0,1:T(8,128)(2,1)}, u32[]{:S(2)}, u32[]{:S(2)}) collective-permute-start(bf16[1024,32]{0,1:T(8,128)(2,1)} %param.22), channel_id=1, source_target_pairs={{0,1},{1,0},{2,3},{3,2},{4,5},{5,4},{6,7},{7,6},{8,9},{9,8},{10,11... | collective-permute-start | bytes 196616 | tf_op jit(solution)/shard_map/ppermute | solution.py:27
  181.1 10.7 %copy-start.23 = (f32[512]{0:T(512)S(1)}, f32[512]{0:T(512)}, u32[]{:S(2)}) copy-start(f32[512]{0:T(512)} %copy-done.22) | copy-start | bytes 6148
  184.7 6.3 %copy-start.5 = (bf16[1024,64]{0,1:T(8,128)(2,1)}, bf16[1024,64]{0,1:T(8,128)(2,1)S(1)}, u32[]{:S(2)}) copy-start(bf16[1024,64]{0,1:T(8,128)(2,1)S(1)} %maximum_select_fusion.3) | copy-start | bytes 393220
  184.8 6.3 %collective-permute-start.3 = (bf16[1024,64]{0,1:T(8,128)(2,1)S(1)}, bf16[1024,64]{0,1:T(8,128)(2,1)S(1)}, u32[]{:S(2)}, u32[]{:S(2)}) collective-permute-start(bf16[1024,64]{0,1:T(8,128)(2,1)S(1)} %maximum_select_fusion.3), channel_id=1, source_target_pairs={{0,2},{2,0},{1,3},{3,1},{4,6},{6,4},{5,7},{7,5},{8,10},{10,8},{9,1... | collective-permute-start | bytes 393224 | tf_op jit(solution)/shard_map/ppermute | solution.py:27
  261.0 21.8 %copy-start.11 = (bf16[512,64]{0,1:T(8,128)(2,1)}, bf16[512,64]{0,1:T(8,128)(2,1)S(1)}, u32[]{:S(2)}) copy-start(bf16[512,64]{0,1:T(8,128)(2,1)S(1)} %get-tuple-element.11) | copy-start | bytes 196612
  286.9 1.5 copy-start.17
  287.5 3.6 copy-start.2
  319.2 3.8 copy-start.16
  319.6 4.5 copy-start.6
  319.8 4.3 copy-start.9
  319.8 4.3 copy-start.20
  324.1 2.6 copy-start.18
  324.1 2.6 copy-start.27
  326.7 2.7 copy-start.13
  326.8 3.1 copy-start.10
  326.8 101.1 %copy-start.24 = (f32[512]{0:T(512)S(1)}, f32[512]{0:T(512)}, u32[]{:S(2)}) copy-start(f32[512]{0:T(512)} %copy-done.22) | copy-start | bytes 6148
  424.3 9.5 %copy-start.7 = (bf16[16,1024]{1,0:T(8,128)(2,1)S(1)}, bf16[16,1024]{1,0:T(8,128)(2,1)}, u32[]{:S(2)}) copy-start(bf16[16,1024]{1,0:T(8,128)(2,1)} %param.14) | copy-start | bytes 98308
  424.3 9.5 %copy-start.21 = (bf16[1024,64]{0,1:T(8,128)(2,1)S(1)}, bf16[1024,64]{0,1:T(8,128)(2,1)}, u32[]{:S(2)}) copy-start(bf16[1024,64]{0,1:T(8,128)(2,1)} %param.24) | copy-start | bytes 393220
  424.3 44.6 %copy-start.8 = (bf16[16,1024]{1,0:T(8,128)(2,1)S(1)}, bf16[16,1024]{1,0:T(8,128)(2,1)}, u32[]{:S(2)}) copy-start(bf16[16,1024]{1,0:T(8,128)(2,1)} %multiply_convert_fusion) | copy-start | bytes 98308
  (4 other events, 4.3 us)
Sparse Core Ops, SparseCore 0:
  10.1 76.3 all-gather.2
  88.7 67.7 all-gather.4
  160.7 119.1 all-reduce.9
  326.8 106.8 reduce-scatter.1
where the time goes:
time: 483 us; the launch traced here: 477 us
  blocking collectives  246 us (51%)
  waiting for transfers between devices  116 us (24%)
  matrix products  60.8 us (13%)
  other arithmetic  18.6 us (4%)
  starting transfers between devices  15.3 us (3%)
  between operations  14.8 us (3%)
  local copies, waits for them, and re-layouts  5.44 us (1%)
    psum x1, blocking collectives, per_device(): low_back_sum = lax.psum(low_back_part, 'col')  94.2 us
    psum x1, blocking collectives, per_device(): grad_rows, low_grad_sum = lax.psum((full_grad, low_grad_part), 'row')  68.1 us
    all_gather x1, waiting for transfers between devices, per_device(): lax.all_gather(hidden, 'col', axis=0, tiled=True)  63.6 us
    psum x1, blocking collectives, per_device(): lax.psum(jnp.sum(hidden_wide * gain_wide[None, :] * normalized_gradient,...  33.8 us
    psum x1, blocking collectives, per_device(): lax.psum(jnp.sum(hidden_all_wide * hidden_all_wide, axis=1), 'row')  33.3 us
    all_gather x1, waiting for transfers between devices, per_device(): lax.all_gather(weighted_own, 'col', axis=0, tiled=True)  30.8 us
    psum x1, waiting for transfers between devices, per_device(): grad_rows, low_grad_sum = lax.psum((full_grad, low_grad_part), 'row')  19 us
    unnamed x1, blocking collectives  16.5 us
  transfers between devices with their start and end apart: 8, of which 5 were waited for; matrix products, arithmetic and copies ran while one was open for 7% of the time, Pallas kernels for 0%

commit v1 on v0

v1 whole, which is shorter than its diff:
```python
import functools
import math

import jax
import jax.numpy as jnp
from jax import lax
from jax.experimental import pallas as pl
from jax.experimental.pallas import tpu as pltpu
from jax.sharding import PartitionSpec as P

MODEL_WIDTH = 16384
HEAD = 128
RANK = 64
GROUP = 4
EPS = 1e-05
CAP = 2.0
BASE = 500000.0
FILL = -1e30
SCALE = HEAD**-0.5
MESH = pl.DeviceIdType.MESH
F32 = jnp.float32
BF16 = jnp.bfloat16
REACH = 4


def nn(a, b):
    return lax.dot_general(a, b, (((1,), (0,)), ((), ())), preferred_element_type=F32)


def nt(a, b):
    return lax.dot_general(a, b, (((1,), (1,)), ((), ())), preferred_element_type=F32)


def tn(a, b):
    return lax.dot_general(a, b, (((0,), (0,)), ((), ())), preferred_element_type=F32)


def remote(src, dst, send, recv, device):
    return pltpu.make_async_remote_copy(
        src_ref=src, dst_ref=dst, send_sem=send, recv_sem=recv,
        device_id=device, device_id_type=MESH,
    )


def kernel(
    R, Z,
    hid, cot, aux_in, gain, wq, qdown, kvt_own, wo, oup, odown, qup,
    igrad, qdown_g, qup_g, odown_g, oup_g,
    h_all, w_all, n_all, aux_all, kvt,
    ssq, part, rx, kvx, kvpart, kvrx, qg_all, kvg_all, att_all, dots,
    own, sib_out, sib_in, hop_out, hop_in, low_all,
    ring_s, ring_r, sib_s, sib_r, ssq_s, ssq_r, aux_s, aux_r, auxsib, kvt_s, kvt_r,
    rs_s, rs_r, kvx_s, kvx_r, kvp_s, kvp_r, qg_s, qg_r, kvg_s, kvg_r, att_s, att_r,
    sg_s, sg_r, hop_s, hop_r, low_s, low_r, lowsib, dot_s, dot_r,
):
    row = lax.axis_index("row")
    col = lax.axis_index("col")
    z = lax.div(col, 2)
    core = lax.rem(col, 2)
    B = hid.shape[0]
    S = 2 * B
    T = S * Z
    D = hid.shape[1]
    H = wo.shape[0]
    heads = H // HEAD
    CH = 4
    counts = {1: Z // 2, -1: Z - 1 - Z // 2}
    dirs = (1, -1)

    def zmod(v):
        return lax.rem(v + 2 * Z, Z)

    def at_z(v):
        return {"col": zmod(v) * 2 + core}

    sibling = {"col": z * 2 + 1 - core}
    pair = z + 1 - 2 * lax.rem(z, 2)

    def peer(k):
        return lax.rem(row + k, R)

    def each(n, f):
        def step(k, carry):
            f(k)
            return carry
        lax.fori_loop(1, n, step, 0)

    def row_copy(src, dst, ss, rs, k):
        return remote(src, dst, ss.at[k], rs, {"row": peer(k)})

    def row_bcast(src, dst_all, ss, rs):
        each(R, lambda k: row_copy(src, dst_all.at[row], ss, rs.at[row], k).start())

    def row_recv(dst_all, rs, ss, k):
        s = peer(k)
        row_copy(dst_all.at[s], dst_all.at[s], ss, rs.at[s], k).wait_recv()

    def row_done(src, dst_all, ss, rs):
        each(R, lambda k: row_copy(src, dst_all.at[row], ss, rs.at[row], k).wait_send())

    barrier = pltpu.get_barrier_semaphore()
    each(R, lambda k: pl.semaphore_signal(
        barrier, inc=1, device_id={"row": peer(k)}, device_id_type=MESH))
    each(Z, lambda k: pl.semaphore_signal(
        barrier, inc=1, device_id=at_z(z + k), device_id_type=MESH))
    pl.semaphore_signal(barrier, inc=1, device_id=sibling, device_id_type=MESH)
    pl.semaphore_signal(
        barrier, inc=1, device_id={"col": pair * 2 + 1 - core}, device_id_type=MESH)

    aux0 = aux_in[...]
    hf = hid[...].astype(F32)
    gf = gain[...].astype(F32)
    w_own = (cot[...].astype(F32) * aux0[:, 6:7]).astype(BF16)
    w_all[z, core] = w_own
    h_all[z, core] = hid[...]
    ssq[row] = jnp.broadcast_to(jnp.sum(hf * hf, axis=1, keepdims=True), (B, 128))
    member = lax.rem(col, GROUP)
    kvt[member] = kvt_own[...]
    pl.semaphore_wait(barrier, R - 1 + Z - 1 + 2)

    arrays = (w_all, h_all)
    started = []

    def ring_send(a, d, ch, t):
        off = t if ch == 0 else (0 if t == 0 else REACH + t)
        block = arrays[a].at[zmod(z - d * off), core]
        target = z + d * (REACH + 1 if ch == 1 and t == 0 else 1)
        i = 0 if d == 1 else 1
        cp = remote(block, block, ring_s.at[a, i, ch, t], ring_r.at[a, i, ch, t], at_z(target))
        cp.start()
        started.append(cp)
        return cp

    sibs = []

    def sib_send(a, i, off):
        block = arrays[a].at[zmod(z + off), core]
        cp = remote(block, block, sib_s.at[a, i], sib_r.at[a, i], sibling)
        cp.start()
        started.append(cp)
        sibs.append(cp)

    def length(d, ch):
        return min(REACH, counts[d]) if ch == 0 else max(counts[d] - REACH, 0)

    flying = {}
    for a in range(2):
        for ch in (1, 0):
            for d in dirs:
                if length(d, ch) > 0:
                    flying[a, d, ch] = ring_send(a, d, ch, 0)
    row_bcast(ssq.at[row], ssq, ssq_s, ssq_r)
    for a in range(2):
        sib_send(a, 0, 0)
    kvt_cp = []
    for i, dev in enumerate((sibling, {"col": pair * 2 + core}, {"col": pair * 2 + 1 - core})):
        cp = remote(kvt.at[member], kvt.at[member], kvt_s.at[i], kvt_r.at[i], dev)
        cp.start()
        kvt_cp.append(cp)

    count = {0: 1, 1: 1}

    def ring_step(t):
        for a in range(2):
            for ch in (0, 1):
                for d in dirs:
                    if t >= length(d, ch):
                        continue
                    flying[a, d, ch].wait_recv()
                    if t + 1 < length(d, ch):
                        flying[a, d, ch] = ring_send(a, d, ch, t + 1)
                    sib_send(a, count[a], -d * (t + 1 + (REACH if ch else 0)))
                    count[a] += 1

    ring_step(0)
    each(R, lambda k: row_recv(ssq, ssq_r, ssq_s, k))
    total = ssq[0]
    for i in range(1, R):
        total = total + ssq[i]
    inv_own = lax.rsqrt(total * (1.0 / MODEL_WIDTH) + EPS)
    lane = lax.broadcasted_iota(jnp.int32, (B, 128), 1)
    hi = inv_own.astype(BF16).astype(F32)
    mid = (inv_own - hi).astype(BF16).astype(F32)
    lo = inv_own - hi - mid
    aux_all[z, core] = jnp.where(
        lane == 0, hi, jnp.where(lane == 1, mid, jnp.where(lane == 2, lo, aux0))
    ).astype(BF16)

    def aux_copy(k):
        return remote(aux_all.at[z, core], aux_all.at[z, core], aux_s.at[k], aux_r.at[z],
                      at_z(z + k))

    each(Z, lambda k: aux_copy(k).start())
    for t in range(1, REACH):
        ring_step(t)

    def aux_recv(k):
        s = zmod(z + k)
        remote(aux_all.at[s, core], aux_all.at[s, core], aux_s.at[k], aux_r.at[s],
               at_z(z + k)).wait_recv()

    each(Z, aux_recv)
    aux_half = remote(aux_all.at[:, core], aux_all.at[:, core], auxsib.at[0], auxsib.at[1], sibling)
    aux_half.start()
    for cp in sibs:
        cp.wait_recv()
    for cp in kvt_cp:
        cp.wait_recv()
    aux_half.wait_recv()

    kv_rows = jnp.concatenate(
        [kvt[g, half * 32:half * 32 + 32, :] for half in range(2) for g in range(GROUP)], axis=0)
    KV0 = 2 * H
    LOW0 = KV0 + 2 * HEAD
    chunks = Z // CH
    rows_c = CH * S

    def rs_copy(p):
        return remote(part.at[p], rx.at[row], rs_s.at[p], rs_r.at[row], {"row": p})

    def project(i, carry):
        q = lax.rem(lax.div(row, CH) + i, chunks)
        first = q * CH
        w = w_all[pl.ds(first, CH)].reshape(rows_c, D)
        h = h_all[pl.ds(first, CH)].reshape(rows_c, D).astype(F32)
        ax = aux_all[pl.ds(first, CH)].reshape(rows_c, 128).astype(F32)
        inv = ax[:, 0:1] + ax[:, 1:2] + ax[:, 2:3]
        n = (h * inv * gf).astype(BF16)
        n_all[pl.ds(first, CH)] = n.reshape(CH, S, D)
        span = pl.ds(first, CH)
        part[span, :, 0:H] = nt(w, wo[...]).astype(BF16).reshape(CH, S, H)
        part[span, :, H:KV0] = nn(n, wq[...]).astype(BF16).reshape(CH, S, H)
        part[span, :, KV0:LOW0] = nt(n, kv_rows).astype(BF16).reshape(CH, S, 2 * HEAD)
        part[span, :, LOW0:LOW0 + 128] = jnp.concatenate(
            [nt(w, oup[...]), nn(n, qdown[...])], axis=1).astype(BF16).reshape(CH, S, 128)
        for m in range(CH):
            p = first + lax.rem(row + m, CH)

            @pl.when(p != row)
            def _():
                rs_copy(p).start()
        return carry

    lax.fori_loop(0, chunks, project, 0)

    ax = aux_all[row].reshape(S, 128).astype(F32)
    pos = ax[:, 3:4] * 64.0 + ax[:, 4:5]
    lane_s = lax.broadcasted_iota(jnp.int32, (S, HEAD), 1)
    half_lane = lax.rem(lane_s, HEAD // 2).astype(F32)
    angle = pos * jnp.exp(half_lane * (-2.0 * math.log(BASE) / HEAD))
    cosine = jnp.cos(angle)
    sine = jnp.where(lane_s < HEAD // 2, -1.0, 1.0) * jnp.sin(angle)

    def swap(x):
        return jnp.concatenate([x[:, HEAD // 2:], x[:, :HEAD // 2]], axis=1)

    def rotate(x):
        return x * cosine + swap(x) * sine

    def unrotate(x):
        return x * cosine - swap(x) * sine

    pick = (lax.broadcasted_iota(jnp.int32, (8, 128), 1) == 5).astype(BF16)
    seg_key = nt(pick, aux_all[...].reshape(T, 128))[0:1, :]
    token = row * S + lax.broadcasted_iota(jnp.int32, (S, T), 0)
    allowed = (ax[:, 5:6] == seg_key) & (lax.broadcasted_iota(jnp.int32, (S, T), 1) <= token)
    allowed = jnp.concatenate([allowed.astype(F32)] * heads, axis=0) > 0.5

    acc = part[row].astype(F32)
    for k in range(1, R):
        row_recv(rx, rs_r, rs_s, k)
        acc = acc + rx[peer(k)].astype(F32)
    low = acc[:, LOW0:LOW0 + 128].astype(BF16)
    kvx[row, :, 0:HEAD] = rotate(acc[:, KV0:KV0 + HEAD]).astype(BF16)
    kvx[row, :, HEAD:2 * HEAD] = acc[:, KV0 + HEAD:LOW0].astype(BF16)
    kvx[row, :, 2 * HEAD:3 * HEAD] = low
    row_bcast(kvx.at[row], kvx, kvx_s, kvx_r)
    dA = (acc[:, 0:H] + 2.0 * nt(low[:, 0:RANK], odown[...])).astype(BF16)
    ql = acc[:, H:KV0] + 2.0 * nn(low[:, RANK:2 * RANK], qup[...])
    queries = jnp.concatenate(
        [rotate(ql[:, i * HEAD:(i + 1) * HEAD]).astype(BF16) for i in range(heads)], axis=0)
    grads = jnp.concatenate([dA[:, i * HEAD:(i + 1) * HEAD] for i in range(heads)], axis=0)
    each(R, lambda k: row_recv(kvx, kvx_r, kvx_s, k))

    keys = kvx[:, :, 0:HEAD].reshape(T, HEAD)
    values = kvx[:, :, HEAD:2 * HEAD].reshape(T, HEAD)
    scores = jnp.where(allowed, nt(queries, keys) * SCALE, FILL)
    shifted = jnp.exp(scores - jnp.max(scores, axis=1, keepdims=True))
    probs = shifted / jnp.sum(shifted, axis=1, keepdims=True)
    narrow = probs.astype(BF16)
    pgrad = nt(grads, values)
    rdot = jnp.sum(probs * pgrad, axis=1, keepdims=True)
    sgrad = (probs * (pgrad - rdot) * SCALE).astype(BF16)
    kvpart[:, :, 0:HEAD] = tn(sgrad, queries).astype(BF16).reshape(R, S, HEAD)
    kvpart[:, :, HEAD:2 * HEAD] = tn(narrow, grads).astype(BF16).reshape(R, S, HEAD)

    def kvp_copy(k):
        return remote(kvpart.at[peer(k)], kvrx.at[row], kvp_s.at[k], kvp_r.at[row],
                      {"row": peer(k)})

    each(R, lambda k: kvp_copy(k).start())
    qg = nn(sgrad, keys)
    for i in range(heads):
        qg_all[row, :, i * HEAD:(i + 1) * HEAD] = unrotate(qg[i * S:(i + 1) * S]).astype(BF16)
    row_bcast(qg_all.at[row], qg_all, qg_s, qg_r)
    att = nn(narrow, values).astype(BF16)
    for i in range(heads):
        att_all[row, :, i * HEAD:(i + 1) * HEAD] = att[i * S:(i + 1) * S]
    kacc = kvpart[row].astype(F32)
    for k in range(1, R):
        row_recv(kvrx, kvp_r, kvp_s, k)
        kacc = kacc + kvrx[peer(k)].astype(F32)
    kvg_all[row, :, 0:HEAD] = unrotate(kacc[:, 0:HEAD]).astype(BF16)
    kvg_all[row, :, HEAD:2 * HEAD] = kacc[:, HEAD:2 * HEAD].astype(BF16)
    row_bcast(kvg_all.at[row], kvg_all, kvg_s, kvg_r)
    row_bcast(att_all.at[row], att_all, att_s, att_r)
    each(R, lambda k: row_recv(qg_all, qg_r, qg_s, k))
    each(R, lambda k: row_recv(kvg_all, kvg_r, kvg_s, k))
    each(R, lambda k: row_recv(att_all, att_r, att_s, k))

    def sg_copy(q):
        span = pl.ds(q * CH, CH)
        return remote(sib_out.at[span], sib_in.at[span], sg_s.at[q], sg_r.at[q], sibling)

    def backward(i, carry):
        q = lax.rem(lax.div(z, CH) + chunks // 2 + i, chunks)
        span = pl.ds(q * CH, CH)
        qrows = qg_all[span].reshape(rows_c, H)
        krows = kvg_all[span].reshape(rows_c, 2 * HEAD)
        arows = att_all[span].reshape(rows_c, H)
        g = nt(qrows, wq[...]) + nn(krows, kv_rows)
        lows = jnp.concatenate([nn(arows, odown[...]), nt(qrows, qup[...])], axis=1)
        g = g.reshape(CH, 2, B, D)
        lows = lows.reshape(CH, 2, B, 128)
        mine = core == 0
        own[span, :, 0:D] = jnp.where(mine, g[:, 0], g[:, 1])
        own[span, :, D:D + 128] = jnp.where(mine, lows[:, 0], lows[:, 1])
        sib_out[span, :, 0:D] = jnp.where(mine, g[:, 1], g[:, 0]).astype(BF16)
        sib_out[span, :, D:D + 128] = jnp.where(mine, lows[:, 1], lows[:, 0]).astype(BF16)
        sg_copy(q).start()
        return carry

    lax.fori_loop(0, chunks, backward, 0)

    def add_sibling(i, carry):
        q = lax.rem(lax.div(z, CH) + chunks // 2 + i, chunks)
        span = pl.ds(q * CH, CH)
        sg_copy(q).wait_recv()
        own[span] = own[span] + sib_in[span].astype(F32)
        return carry

    lax.fori_loop(0, chunks, add_sibling, 0)

    hops = {}

    def hop(d, ch, t):
        i = 0 if d == 1 else 1
        far = ch == 1 and t == REACH - 1
        return remote(hop_out.at[i, ch, t], hop_in.at[i, ch, t], hop_s.at[i, ch, t],
                      hop_r.at[i, ch, t], at_z(z + d * (REACH + 1 if far else 1)))

    for t in range(REACH):
        for ch in (1, 0):
            for d in dirs:
                delta = REACH - t + (REACH if ch else 0)
                last = REACH if ch == 0 else counts[d]
                if delta > last:
                    continue
                i = 0 if d == 1 else 1
                term = own[zmod(z + d * delta)]
                if delta < last:
                    hops[d, ch, t - 1].wait_recv()
                    term = term + hop_in[i, ch, t - 1].astype(F32)
                hop_out[i, ch, t] = term.astype(BF16)
                hops[d, ch, t] = hop(d, ch, t)
                hops[d, ch, t].start()

    lows_all = kvx[:, :, 2 * HEAD:3 * HEAD].reshape(T, 128)
    qup_g[...] = 2.0 * tn(lows_all, qg_all[...].reshape(T, H))[RANK:2 * RANK]
    odown_g[...] = 2.0 * tn(att_all[...].reshape(T, H), lows_all[:, 0:RANK])

    final = own[z]
    for ch in (0, 1):
        for d in dirs:
            if length(d, ch) > 0:
                hops[d, ch, REACH - 1].wait_recv()
                final = final + hop_in[0 if d == 1 else 1, ch, REACH - 1].astype(F32)

    low_all[z, core] = final[:, D:D + 128].astype(BF16)

    def low_copy(k):
        return remote(low_all.at[z, core], low_all.at[z, core], low_s.at[k], low_r.at[z],
                      at_z(z + k))

    each(Z, lambda k: low_copy(k).start())
    low_back = final[:, D + RANK:D + 2 * RANK].astype(BF16)
    ngrad = final[:, 0:D] + 2.0 * nt(low_back, qdown[...])
    dots[row] = jnp.broadcast_to(
        jnp.sum(hf * gf * ngrad, axis=1, keepdims=True), (B, 128))
    row_bcast(dots.at[row], dots, dot_s, dot_r)

    def low_recv(k):
        s = zmod(z + k)
        remote(low_all.at[s, core], low_all.at[s, core], low_s.at[k], low_r.at[s],
               at_z(z + k)).wait_recv()

    each(Z, low_recv)
    low_half = remote(low_all.at[:, core], low_all.at[:, core], lowsib.at[0], lowsib.at[1], sibling)
    low_half.start()
    each(R, lambda k: row_recv(dots, dot_r, dot_s, k))
    dsum = dots[0]
    for i in range(1, R):
        dsum = dsum + dots[i]
    inv = inv_own[:, 0:1]
    igrad[...] = (
        w_own.astype(F32) + inv * gf * ngrad
        - hf * (inv * inv * inv * dsum[:, 0:1] * (1.0 / MODEL_WIDTH)))
    low_half.wait_recv()
    lb = low_all[...].reshape(T, 128)
    oup_g[...] = 2.0 * tn(lb, w_all[...].reshape(T, D))[0:RANK]
    qdown_g[...] = 2.0 * tn(n_all[...].reshape(T, D), lb)[:, RANK:2 * RANK]

    for cp in started:
        cp.wait_send()
    for cp in kvt_cp:
        cp.wait_send()
    row_done(ssq.at[row], ssq, ssq_s, ssq_r)
    each(Z, lambda k: aux_copy(k).wait_send())
    aux_half.wait_send()
    each(R, lambda k: rs_copy(peer(k)).wait_send())
    row_done(kvx.at[row], kvx, kvx_s, kvx_r)
    each(R, lambda k: kvp_copy(k).wait_send())
    row_done(qg_all.at[row], qg_all, qg_s, qg_r)
    row_done(kvg_all.at[row], kvg_all, kvg_s, kvg_r)
    row_done(att_all.at[row], att_all, att_s, att_r)
    for q in range(chunks):
        sg_copy(q).wait_send()
    for cp in hops.values():
        cp.wait_send()
    each(Z, lambda k: low_copy(k).wait_send())
    low_half.wait_send()
    row_done(dots.at[row], dots, dot_s, dot_r)


def per_device(
    hidden, cotangent, importance, positions, segments, norm_gain, query_weight_matrix,
    key_weight, value_weight_matrix, output_weight_matrix, query_down_factor, query_up_factor,
    output_down_factor, out_up,
):
    R = lax.axis_size("row")
    C = lax.axis_size("col")
    Z = C // 2
    B, D = hidden.shape
    H = query_weight_matrix.shape[1]
    S = 2 * B
    T = B * C
    W = 2 * H + 2 * HEAD + 128
    lane = jnp.arange(128)[None, :]
    cols = (
        (3, (positions // 64).astype(F32)),
        (4, (positions % 64).astype(F32)),
        (5, segments.astype(F32)),
        (6, jnp.minimum(importance.astype(F32), CAP)),
    )
    aux = jnp.zeros((B, 128), F32)
    for i, v in cols:
        aux = jnp.where(lane == i, v[:, None], aux)
    kvt = jnp.concatenate([key_weight, value_weight_matrix], axis=1).T
    vmem = pl.BlockSpec(memory_space=pltpu.VMEM)
    dma = pltpu.SemaphoreType.DMA
    outs = (
        jax.ShapeDtypeStruct((B, D), F32),
        jax.ShapeDtypeStruct((D, RANK), F32),
        jax.ShapeDtypeStruct((RANK, H), F32),
        jax.ShapeDtypeStruct((H, RANK), F32),
        jax.ShapeDtypeStruct((RANK, D), F32),
    )
    scratch = [
        pltpu.VMEM((Z, 2, B, D), BF16),
        pltpu.VMEM((Z, 2, B, D), BF16),
        pltpu.VMEM((Z, S, D), BF16),
        pltpu.VMEM((Z, 2, B, 128), BF16),
        pltpu.VMEM((GROUP, 64, D), BF16),
        pltpu.VMEM((R, B, 128), F32),
        pltpu.VMEM((R, S, W), BF16),
        pltpu.VMEM((R, S, W), BF16),
        pltpu.VMEM((R, S, 3 * HEAD), BF16),
        pltpu.VMEM((R, S, 2 * HEAD), BF16),
        pltpu.VMEM((R, S, 2 * HEAD), BF16),
        pltpu.VMEM((R, S, H), BF16),
        pltpu.VMEM((R, S, 2 * HEAD), BF16),
        pltpu.VMEM((R, S, H), BF16),
        pltpu.VMEM((R, B, 128), F32),
        pltpu.VMEM((Z, B, D + 128), F32),
        pltpu.VMEM((Z, B, D + 128), BF16),
        pltpu.VMEM((Z, B, D + 128), BF16),
        pltpu.VMEM((2, 2, REACH, B, D + 128), BF16),
        pltpu.VMEM((2, 2, REACH, B, D + 128), BF16),
        pltpu.VMEM((Z, 2, B, 128), BF16),
        dma((2, 2, 2, REACH)), dma((2, 2, 2, REACH)),
        dma((2, Z)), dma((2, Z)),
        dma((R,)), dma((R,)),
        dma((Z,)), dma((Z,)), dma((2,)),
        dma((3,)), dma((3,)),
        dma((R,)), dma((R,)),
        dma((R,)), dma((R,)),
        dma((R,)), dma((R,)),
        dma((R,)), dma((R,)),
        dma((R,)), dma((R,)),
        dma((R,)), dma((R,)),
        dma((Z,)), dma((Z,)),
        dma((2, 2, REACH)), dma((2, 2, REACH)),
        dma((Z,)), dma((Z,)), dma((2,)),
        dma((R,)), dma((R,)),
    ]
    return tuple(pl.pallas_call(
        functools.partial(kernel, R, Z),
        out_shape=outs,
        in_specs=[vmem] * 11,
        out_specs=[vmem] * 5,
        scratch_shapes=scratch,
        compiler_params=pltpu.CompilerParams(
            collective_id=0, has_side_effects=True, vmem_limit_bytes=56 * 1024 * 1024),
        name="attention_backward",
    )(
        hidden, cotangent, aux, norm_gain.reshape(1, D), query_weight_matrix,
        query_down_factor, kvt.reshape(2 * (H // 16), D), output_weight_matrix, out_up,
        output_down_factor, query_up_factor,
    ))


def solution(mesh):
    placed = (
        P("col", "row"), P("col", "row"), P("col"), P("col"), P("col"), P("row"),
        P("row", "col"), P("row", "col"), P("row", "col"), P("col", "row"),
        P("row", None), P(None, "col"), P("col", None), P(None, "row"),
    )
    return jax.shard_map(
        per_device,
        mesh=mesh,
        in_specs=placed,
        out_specs=(P("col", "row"), P("row", None), P(None, "col"), P("col", None), P(None, "row")),
        check_vma=False,
    )
```

time: 483 us -> 149 us (0.31); the launches traced: 477 us -> 149 us
  blocking collectives: 246 us -> 0 us
  Pallas kernels: 0 us -> 136 us
  waiting for transfers between devices: 116 us -> 0 us
  matrix products: 60.8 us -> 0 us
  other arithmetic: 18.6 us -> 2.93 us
  starting transfers between devices: 15.3 us -> 0 us
  between operations: 14.8 us -> 0.68 us
    psum x4 -> x0, blocking collectives: 229 us -> none  [the longest x1 94.2 us: per_device(): low_back_sum = lax.psum(low_back_part, 'col')]
    pallas_call x0 -> x1, Pallas kernels: none -> 136 us  [per_device(): pl.pallas_call(functools.partial(kernel, R, Z), out_shape=outs, in_specs=...]
    all_gather x2 -> x0, waiting for transfers between devices: 94.5 us -> none  [the longest x1 63.6 us: per_device(): lax.all_gather(hidden, 'col', axis=0, tiled=True)]
    dot_general x23 -> x0, matrix products: 55.1 us -> none  [the longest x5 10 us: matrix_product(): return jnp.dot(left, right, preferred_element_type=jnp.float32)]
    psum x1 -> x0, waiting for transfers between devices: 19 us -> none  [per_device(): grad_rows, low_grad_sum = lax.psum((full_grad, low_grad_part), 'row')]
    unnamed x1 -> x0, blocking collectives: 16.5 us -> none
    ppermute x4 -> x0, starting transfers between devices: 15.1 us -> none  [from_partner(): return lax.ppermute(block, axis, route)]
    sub x1 -> x0, matrix products: 5.66 us -> none  [per_device(): shifted = jnp.exp(scores - jnp.max(scores, axis=2, keepdims=True))]
  transfers between devices with their start and end apart: 8 -> 0, of which waited for: 5 -> 0; matrix products, arithmetic and copies ran while one was open for 7% -> 0% of each run, Pallas kernels for 0% -> 0%
where the time goes in v1:
time: 149 us
  Pallas kernels  136 us (91%)
  local copies, waits for them, and re-layouts  8.69 us (6%)
  other arithmetic  2.93 us (2%)
    pallas_call x1, Pallas kernels, per_device(): pl.pallas_call(functools.partial(kernel, R, Z), out_shape=outs, in_specs=...  136 us
    unnamed x21, local copies, waits for them, and re-layouts  4.41 us
    pallas_call x2, local copies, waits for them, and re-layouts, per_device(): pl.pallas_call(functools.partial(kernel, R, Z), out_shape=outs, in_specs=...  3.69 us

profile of v1, /device:TPU:1, one launch (start us, length us, event | category | flops | bytes accessed | tf_op | source)
XLA Modules:
  0.0 148.7 jit_solution(15942487304317742422)
XLA Ops:
  0.6 0.0 copy-start.6
  0.6 0.7 convert_minimum_fusion
  1.3 0.0 copy-done.6
  1.3 0.0 copy-start.7
  1.3 0.6 copy-done.7
  2.0 0.0 copy-start.5
  2.0 0.7 select_select_fusion.aux_in
  2.7 0.0 copy-done.5
  2.7 0.6 reshape.37.gain
  3.3 0.0 copy-start.3
  3.3 1.6 %maximum_bitcast_fusion.kvt_own = bf16[64,1024]{1,0:T(8,128)(2,1)} fusion(bf16[1024,32]{0,1:T(8,128)(2,1)} %param.22, bf16[1024,32]{0,1:T(8,128)(2,1)} %param.21), kind=kLoop, calls=%fused_computation | loop fusion | flops 262144 | bytes 262144 | tf_op jit(solution)/shard_map/transpose | solution.py:468
  4.9 0.0 copy-done.3
  4.9 0.0 copy-start.1
  4.9 0.8 copy.20.odown
  5.6 0.1 copy-done.1
  5.8 0.8 copy.19.qdown
  6.6 136.4 %attention_backward.1 = (f32[16,1024]{1,0:T(8,128)}, f32[1024,64]{1,0:T(8,128)}, f32[64,512]{1,0:T(8,128)}, f32[512,64]{1,0:T(8,128)}, f32[64,1024]{1,0:T(8,128)}) custom-call(bf16[16,1024]{1,0:T(8,128)(2,1)} %hid.1, bf16[16,1024]{1,0:T(8,128)(2,1)} %cot.1, f32[16,128]{1,0:T(8,128)} %select_select_fusion.aux_in, bf16[1,1024]{1,0:T(2,128)(2,1)} %reshape.37.gain, ...), custom_call_target="tpu_custom_call" | custom-call | tf_op jit(solution)/shard_map/attention_backward/pallas_call | solution.py:516
  143.0 1.7 %copy.22 = f32[512,64]{0,1:T(8,128)} copy(f32[512,64]{1,0:T(8,128)} %get-tuple-element.8) | data formatting | bytes 262144 | tf_op jit(solution)/shard_map/attention_backward/pallas_call | solution.py:516
  144.7 0.0 copy-start.4
  144.7 0.0 copy-start.2
  144.7 2.0 %copy.21 = f32[1024,64]{0,1:T(8,128)} copy(f32[1024,64]{1,0:T(8,128)} %get-tuple-element.6) | data formatting | bytes 524288 | tf_op jit(solution)/shard_map/attention_backward/pallas_call | solution.py:516
  146.7 0.0 copy-done.4
  146.7 0.0 copy-start
  146.7 0.6 copy.26
  147.3 0.0 copy-done.2
  147.3 0.7 copy.27
  148.0 0.0 copy-done
  148.0 0.7 copy.28
  (4 shorter events, 0.0 us)
Async XLA Ops:
  0.6 0.7 copy-start.6
  1.3 0.7 copy-start.7
  2.0 0.7 copy-start.5
  3.3 1.6 %copy-start.3 = (bf16[512,64]{0,1:T(8,128)(2,1)S(1)}, bf16[512,64]{0,1:T(8,128)(2,1)}, u32[]{:S(2)}) copy-start(bf16[512,64]{0,1:T(8,128)(2,1)} %param.26) | copy-start | bytes 196612
  4.9 0.9 copy-start.1
  144.7 2.0 %copy-start.4 = (f32[16,1024]{1,0:T(8,128)S(1)}, f32[16,1024]{1,0:T(8,128)}, u32[]{:S(2)}) copy-start(f32[16,1024]{1,0:T(8,128)} %get-tuple-element.21) | copy-start | bytes 196612
  144.7 2.6 %copy-start.2 = (f32[64,512]{1,0:T(8,128)S(1)}, f32[64,512]{1,0:T(8,128)}, u32[]{:S(2)}) copy-start(f32[64,512]{1,0:T(8,128)} %get-tuple-element.23) | copy-start | bytes 393220
  146.7 1.3 copy-start

commit v2 on v1

v2 whole, which is shorter than its diff:
```python
import functools
import math

import jax
import jax.numpy as jnp
from jax import lax
from jax.experimental import pallas as pl
from jax.experimental.pallas import tpu as pltpu
from jax.sharding import PartitionSpec as P

MODEL_WIDTH = 16384
HEAD = 128
RANK = 64
GROUP = 4
EPS = 1e-05
CAP = 2.0
BASE = 500000.0
FILL = -1e30
SCALE = HEAD**-0.5
MESH = pl.DeviceIdType.MESH
F32 = jnp.float32
BF16 = jnp.bfloat16
REACH = 4


def nn(a, b):
    return lax.dot_general(a, b, (((1,), (0,)), ((), ())), preferred_element_type=F32)


def nt(a, b):
    return lax.dot_general(a, b, (((1,), (1,)), ((), ())), preferred_element_type=F32)


def tn(a, b):
    return lax.dot_general(a, b, (((0,), (0,)), ((), ())), preferred_element_type=F32)


def remote(src, dst, send, recv, device):
    return pltpu.make_async_remote_copy(
        src_ref=src, dst_ref=dst, send_sem=send, recv_sem=recv,
        device_id=device, device_id_type=MESH,
    )


def kernel(
    R, Z,
    hid, cot, imp, posn, segm, gain, wq, qdown_t, kw_t, vw_t, wo, oup, odown_t, qup,
    igrad, qdown_g, qup_g, odown_g, oup_g,
    h_all, w_all, n_all, aux_all, kvt,
    ssq, part_w, rx_w, part_kv, rx_kv, part_q, rx_q, kvx, lowx, kvpart, kvrx,
    qg_all, kvg_all, att_all, dots,
    lown, lowz, low_all, gq, own, sib_out, sib_in, hop_out, hop_in,
    ring_s, ring_r, sib_s, sib_r, ssq_s, ssq_r, aux_s, aux_r, auxsib, kvt_s, kvt_r,
    rsw_s, rsw_r, rsk_s, rsk_r, rsq_s, rsq_r, kvx_s, kvx_r, lowx_s, lowx_r,
    kvp_s, kvp_r, qg_s, qg_r, kvg_s, kvg_r, att_s, att_r,
    lowp, lowz_s, lowz_r, low_s, low_r, lowsib, sg_s, sg_r, hop_s, hop_r, dot_s, dot_r,
):
    row = lax.axis_index("row")
    col = lax.axis_index("col")
    z = lax.div(col, 2)
    core = lax.rem(col, 2)
    B, D = hid.shape
    S = 2 * B
    T = S * Z
    H = wo.shape[0]
    heads = H // HEAD
    counts = {1: Z // 2, -1: Z - 1 - Z // 2}
    dirs = (1, -1)
    drains = []

    def zmod(v):
        return lax.rem(v + 2 * Z, Z)

    def at_z(v):
        return {"col": zmod(v) * 2 + core}

    sibling = {"col": z * 2 + 1 - core}
    pair = z + 1 - 2 * lax.rem(z, 2)

    def peer(k):
        return lax.rem(row + k, R)

    def each(n, f):
        def step(k, carry):
            f(k)
            return carry
        lax.fori_loop(1, n, step, 0)

    def start(cp):
        cp.start()
        drains.append(cp.wait_send)
        return cp

    def row_copy(src, dst, ss, rs, k):
        return remote(src, dst, ss.at[k], rs, {"row": peer(k)})

    def row_bcast(src, dst_all, ss, rs):
        def one(k):
            return row_copy(src, dst_all.at[row], ss, rs.at[row], k)
        each(R, lambda k: one(k).start())
        drains.append(lambda: each(R, lambda k: one(k).wait_send()))

    def row_recv(dst_all, rs, ss, k):
        s = peer(k)
        row_copy(dst_all.at[s], dst_all.at[s], ss, rs.at[s], k).wait_recv()

    def z_bcast(src, dst_of, ss, rs):
        def one(k):
            return remote(src, dst_of(z), ss.at[k], rs.at[z], at_z(z + k))
        each(Z, lambda k: one(k).start())
        drains.append(lambda: each(Z, lambda k: one(k).wait_send()))

    def z_recv(dst_of, ss, rs):
        def one(k):
            s = zmod(z + k)
            remote(dst_of(s), dst_of(s), ss.at[k], rs.at[s], at_z(z + k)).wait_recv()
        each(Z, one)

    barrier = pltpu.get_barrier_semaphore()
    each(R, lambda k: pl.semaphore_signal(
        barrier, inc=1, device_id={"row": peer(k)}, device_id_type=MESH))
    each(Z, lambda k: pl.semaphore_signal(
        barrier, inc=1, device_id=at_z(z + k), device_id_type=MESH))
    pl.semaphore_signal(barrier, inc=1, device_id=sibling, device_id_type=MESH)
    pl.semaphore_signal(
        barrier, inc=1, device_id={"col": pair * 2 + 1 - core}, device_id_type=MESH)

    diagonal = (lax.broadcasted_iota(jnp.int32, (B, B), 0)
                == lax.broadcasted_iota(jnp.int32, (B, B), 1))

    def column(v):
        return jnp.sum(jnp.where(diagonal, v.reshape(1, B), 0.0), axis=1, keepdims=True)

    hf = hid[...].astype(F32)
    gf = gain[...].astype(F32).reshape(1, D)
    w_own = (cot[...].astype(F32)
             * column(jnp.minimum(imp[...].astype(F32), CAP))).astype(BF16)
    w_all[z, core] = w_own
    h_all[z, core] = hid[...]
    ssq[row] = jnp.broadcast_to(jnp.sum(hf * hf, axis=1, keepdims=True), (B, 128))
    member = lax.rem(col, GROUP)
    kvt[0, member] = kw_t[...]
    kvt[1, member] = vw_t[...]
    pl.semaphore_wait(barrier, R - 1 + Z - 1 + 2)

    arrays = (w_all, h_all)

    def length(d, ch):
        return min(REACH, counts[d]) if ch == 0 else max(counts[d] - REACH, 0)

    def ring_send(a, d, ch, t):
        off = t if ch == 0 else (0 if t == 0 else REACH + t)
        block = arrays[a].at[zmod(z - d * off), core]
        target = z + d * (REACH + 1 if ch == 1 and t == 0 else 1)
        i = 0 if d == 1 else 1
        return start(remote(
            block, block, ring_s.at[a, i, ch, t], ring_r.at[a, i, ch, t], at_z(target)))

    halves = {}

    def sib_send(a, t, i, off):
        block = arrays[a].at[zmod(z + off), core]
        cp = start(remote(block, block, sib_s.at[a, t, i], sib_r.at[a, t, i], sibling))
        halves.setdefault((a, t), []).append(cp)

    flying = {}
    for a in range(2):
        for ch in (1, 0):
            for d in dirs:
                if length(d, ch) > 0:
                    flying[a, d, ch] = ring_send(a, d, ch, 0)
    row_bcast(ssq.at[row], ssq, ssq_s, ssq_r)
    for a in range(2):
        sib_send(a, REACH - 1, 3, 0)

    def ring_step(t):
        for a in range(2):
            i = 0
            for ch in (1, 0):
                for d in dirs:
                    if t >= length(d, ch):
                        continue
                    flying[a, d, ch].wait_recv()
                    if t + 1 < length(d, ch):
                        flying[a, d, ch] = ring_send(a, d, ch, t + 1)
                    sib_send(a, t, i, -d * (t + 1 + (REACH if ch else 0)))
                    i += 1

    def chips_of(t):
        found = [-d * (t + 1 + (REACH if ch else 0))
                 for ch in (1, 0) for d in dirs if t < length(d, ch)]
        return found + [0] if t == REACH - 1 else found

    groups = [chips_of(t) for t in range(REACH)]

    kvt_cp = []
    for i, dev in enumerate((sibling, {"col": pair * 2 + core}, {"col": pair * 2 + 1 - core})):
        for half in range(2):
            kvt_cp.append(start(remote(
                kvt.at[half, member], kvt.at[half, member], kvt_s.at[i, half],
                kvt_r.at[i, half], dev)))
    ring_step(0)
    each(R, lambda k: row_recv(ssq, ssq_r, ssq_s, k))
    total = ssq[0]
    for i in range(1, R):
        total = total + ssq[i]
    inv_own = lax.rsqrt(total * (1.0 / MODEL_WIDTH) + EPS)
    lane = lax.broadcasted_iota(jnp.int32, (B, 128), 1)
    hi = inv_own.astype(BF16).astype(F32)
    mid = (inv_own - hi).astype(BF16).astype(F32)
    lo = inv_own - hi - mid
    p_own = posn[...]
    p_hi = lax.div(p_own, 64)
    tile = jnp.where(lane == 0, hi, jnp.where(lane == 1, mid, lo))
    for i, v in ((3, p_hi), (4, p_own - p_hi * 64), (5, segm[...])):
        tile = jnp.where(lane == i, column(v.astype(F32)), tile)
    aux_all[z, core] = tile.astype(BF16)
    z_bcast(aux_all.at[z, core], lambda s: aux_all.at[s, core], aux_s, aux_r)

    def rs_copy(src, dst, ss, rs, p):
        return remote(src.at[p], dst.at[row], ss.at[p], rs.at[row], {"row": p})

    def rs_send(group, src, dst, ss, rs):
        n = len(group)
        for m in range(n):
            turn = lax.rem(row + m, n)
            delta = group[0]
            for i in range(1, n):
                delta = jnp.where(turn == i, group[i], delta)
            p = zmod(z + delta)

            @pl.when(p != row)
            def _():
                rs_copy(src, dst, ss, rs, p).start()

    def rs_drain(src, dst, ss, rs):
        drains.append(lambda: each(R, lambda k: rs_copy(src, dst, ss, rs, peer(k)).wait_send()))

    def rows_of(ref, group, width):
        return jnp.concatenate(
            [ref[zmod(z + o)].reshape(S, width) for o in group], axis=0)

    def store(ref, group, value, at=slice(None)):
        for i, o in enumerate(group):
            ref[zmod(z + o), :, at] = value[i * S:(i + 1) * S]

    def project_w(t):
        g = groups[t]
        for cp in halves[0, t]:
            cp.wait_recv()
        store(part_w, g, nt(rows_of(w_all, g, D), wo[...]).astype(BF16))
        rs_send(g, part_w, rx_w, rsw_s, rsw_r)

    def project_kv(t):
        g = groups[t]
        for cp in halves[1, t]:
            cp.wait_recv()
        ax = rows_of(aux_all, g, 128).astype(F32)
        h = rows_of(h_all, g, D).astype(F32)
        n = (h * (ax[:, 0:1] + ax[:, 1:2] + ax[:, 2:3]) * gf).astype(BF16)
        store(n_all, g, n)
        store(part_kv, g, nt(n, kvt[...].reshape(2 * HEAD, D)).astype(BF16), slice(0, 2 * HEAD))
        store(part_kv, g, jnp.concatenate(
            [nt(rows_of(w_all, g, D), oup[...]), nt(n, qdown_t[...])], axis=1).astype(BF16),
            slice(2 * HEAD, 3 * HEAD))
        rs_send(g, part_kv, rx_kv, rsk_s, rsk_r)

    def project_q(t):
        g = groups[t]
        store(part_q, g, nn(rows_of(n_all, g, D), wq[...]).astype(BF16))
        rs_send(g, part_q, rx_q, rsq_s, rsq_r)

    ring_step(1)
    project_w(0)
    ring_step(2)
    project_w(1)
    z_recv(lambda s: aux_all.at[s, core], aux_s, aux_r)
    aux_half = start(remote(
        aux_all.at[:, core], aux_all.at[:, core], auxsib.at[0], auxsib.at[1], sibling))
    ring_step(3)
    project_w(2)
    aux_half.wait_recv()
    for cp in kvt_cp:
        cp.wait_recv()
    for t in range(3):
        project_kv(t)
    project_w(3)
    project_kv(3)
    for t in range(4):
        project_q(t)
    rs_drain(part_w, rx_w, rsw_s, rsw_r)
    rs_drain(part_kv, rx_kv, rsk_s, rsk_r)
    rs_drain(part_q, rx_q, rsq_s, rsq_r)

    ax = aux_all[row].reshape(S, 128).astype(F32)
    pos = ax[:, 3:4] * 64.0 + ax[:, 4:5]
    lane_s = lax.broadcasted_iota(jnp.int32, (S, HEAD), 1)
    half_lane = lax.rem(lane_s, HEAD // 2).astype(F32)
    angle = pos * jnp.exp(half_lane * (-2.0 * math.log(BASE) / HEAD))
    cosine = jnp.cos(angle)
    sine = jnp.where(lane_s < HEAD // 2, -1.0, 1.0) * jnp.sin(angle)

    def swap(x):
        return jnp.concatenate([x[:, HEAD // 2:], x[:, :HEAD // 2]], axis=1)

    def rotate(x):
        return x * cosine + swap(x) * sine

    def unrotate(x):
        return x * cosine - swap(x) * sine

    pick = (lax.broadcasted_iota(jnp.int32, (8, 128), 1) == 5).astype(BF16)
    seg_key = nt(pick, aux_all[...].reshape(T, 128))[0:1, :]
    token = row * S + lax.broadcasted_iota(jnp.int32, (S, T), 0)
    allowed = (ax[:, 5:6] == seg_key) & (lax.broadcasted_iota(jnp.int32, (S, T), 1) <= token)
    allowed = jnp.concatenate([allowed.astype(F32)] * heads, axis=0) > 0.5

    def rs_sum(part, rx, ss, rs):
        acc = part[row].astype(F32)
        for k in range(1, R):
            row_recv(rx, rs, ss, k)
            acc = acc + rx[peer(k)].astype(F32)
        return acc

    dA = rs_sum(part_w, rx_w, rsw_s, rsw_r)
    kvl = rs_sum(part_kv, rx_kv, rsk_s, rsk_r)
    kvx[row, :, 0:HEAD] = rotate(kvl[:, 0:HEAD]).astype(BF16)
    kvx[row, :, HEAD:2 * HEAD] = kvl[:, HEAD:2 * HEAD].astype(BF16)
    row_bcast(kvx.at[row], kvx, kvx_s, kvx_r)
    low = kvl[:, 2 * HEAD:3 * HEAD].astype(BF16)
    lowx[row] = low
    row_bcast(lowx.at[row], lowx, lowx_s, lowx_r)
    dA = (dA + 2.0 * nn(low[:, 0:RANK], odown_t[...])).astype(BF16)
    grads = jnp.concatenate([dA[:, i * HEAD:(i + 1) * HEAD] for i in range(heads)], axis=0)
    ql = 2.0 * nn(low[:, RANK:2 * RANK], qup[...])
    ql = ql + rs_sum(part_q, rx_q, rsq_s, rsq_r)
    queries = jnp.concatenate(
        [rotate(ql[:, i * HEAD:(i + 1) * HEAD]).astype(BF16) for i in range(heads)], axis=0)
    each(R, lambda k: row_recv(kvx, kvx_r, kvx_s, k))

    keys = kvx[:, :, 0:HEAD].reshape(T, HEAD)
    values = kvx[:, :, HEAD:2 * HEAD].reshape(T, HEAD)
    scores = jnp.where(allowed, nt(queries, keys) * SCALE, FILL)
    shifted = jnp.exp(scores - jnp.max(scores, axis=1, keepdims=True))
    probs = shifted / jnp.sum(shifted, axis=1, keepdims=True)
    narrow = probs.astype(BF16)
    pgrad = nt(grads, values)
    rdot = jnp.sum(probs * pgrad, axis=1, keepdims=True)
    sgrad = (probs * (pgrad - rdot) * SCALE).astype(BF16)
    kvpart[:, :, 0:HEAD] = tn(sgrad, queries).astype(BF16).reshape(R, S, HEAD)
    kvpart[:, :, HEAD:2 * HEAD] = tn(narrow, grads).astype(BF16).reshape(R, S, HEAD)

    def kvp_copy(k):
        return remote(kvpart.at[peer(k)], kvrx.at[row], kvp_s.at[k], kvp_r.at[row],
                      {"row": peer(k)})

    each(R, lambda k: kvp_copy(k).start())
    drains.append(lambda: each(R, lambda k: kvp_copy(k).wait_send()))
    qg = nn(sgrad, keys)
    for i in range(heads):
        qg_all[row, :, i * HEAD:(i + 1) * HEAD] = unrotate(qg[i * S:(i + 1) * S]).astype(BF16)
    row_bcast(qg_all.at[row], qg_all, qg_s, qg_r)
    att = nn(narrow, values).astype(BF16)
    for i in range(heads):
        att_all[row, :, i * HEAD:(i + 1) * HEAD] = att[i * S:(i + 1) * S]

    inner = jnp.concatenate(
        [nt(att_all[row], odown_t[...]), nt(qg_all[row], qup[...])], axis=1)
    lown[0] = jnp.where(core == 0, inner[0:B], inner[B:S])
    lown[1] = jnp.where(core == 0, inner[B:S], inner[0:B])
    low_pair = start(remote(lown.at[1], lown.at[2], lowp.at[0], lowp.at[1], sibling))
    kacc = rs_sum(kvpart, kvrx, kvp_s, kvp_r)
    kvg_all[row, :, 0:HEAD] = unrotate(kacc[:, 0:HEAD]).astype(BF16)
    kvg_all[row, :, HEAD:2 * HEAD] = kacc[:, HEAD:2 * HEAD].astype(BF16)
    row_bcast(kvg_all.at[row], kvg_all, kvg_s, kvg_r)
    low_pair.wait_recv()
    lowz[z] = lown[0] + lown[2]
    z_bcast(lowz.at[z], lambda s: lowz.at[s], lowz_s, lowz_r)
    row_bcast(att_all.at[row], att_all, att_s, att_r)

    each(R, lambda k: row_recv(qg_all, qg_r, qg_s, k))
    order = list(reversed(range(REACH)))
    for t in order:
        gq[t, 0:len(groups[t]) * S] = nt(rows_of(qg_all, groups[t], H), wq[...])
    z_recv(lambda s: lowz.at[s], lowz_s, lowz_r)
    inner = lowz[0]
    for i in range(1, Z):
        inner = inner + lowz[i]
    low_all[row, core] = inner.astype(BF16)
    row_bcast(low_all.at[row, core], low_all.at[:, core], low_s, low_r)
    each(R, lambda k: row_recv(kvg_all, kvg_r, kvg_s, k))

    def backward(t):
        g = groups[t]
        value = gq[t, 0:len(g) * S] + nn(
            rows_of(kvg_all, g, 2 * HEAD), kvt[...].reshape(2 * HEAD, D))
        value = value.reshape(len(g), 2, B, D)
        mine = core == 0
        sib_out[t, 0:len(g)] = jnp.where(mine, value[:, 1], value[:, 0]).astype(BF16)
        cp = start(remote(sib_out.at[t, pl.ds(0, len(g))], sib_in.at[t, pl.ds(0, len(g))],
                          sg_s.at[t], sg_r.at[t], sibling))
        own[t, 0:len(g)] = jnp.where(mine, value[:, 0], value[:, 1])
        return cp

    hops = {}

    def hop(d, ch, t):
        i = 0 if d == 1 else 1
        far = ch == 1 and t == REACH - 1
        return remote(hop_out.at[i, ch, t], hop_in.at[i, ch, t], hop_s.at[i, ch, t],
                      hop_r.at[i, ch, t], at_z(z + d * (REACH + 1 if far else 1)))

    def hop_step(t, cp):
        u = REACH - 1 - t
        cp.wait_recv()
        for ch in (1, 0):
            for d in dirs:
                delta = u + 1 + (REACH if ch else 0)
                last = REACH if ch == 0 else counts[d]
                if delta > last:
                    continue
                i = 0 if d == 1 else 1
                slot = groups[u].index(d * delta if d * delta in groups[u] else -d * delta)
                term = own[u, slot] + sib_in[u, slot].astype(F32)
                if delta < last:
                    hops[d, ch, t - 1].wait_recv()
                    term = term + hop_in[i, ch, t - 1].astype(F32)
                hop_out[i, ch, t] = term.astype(BF16)
                hops[d, ch, t] = start(hop(d, ch, t))

    sibs = {}
    for t, u in enumerate(order):
        sibs[t] = backward(u)
        if t > 0:
            hop_step(t - 1, sibs[t - 1])
    own_slot = groups[REACH - 1].index(0)
    final = own[REACH - 1, own_slot] + sib_in[REACH - 1, own_slot].astype(F32)
    low_all_row = low_all.at[:, core]
    each(R, lambda k: row_recv(low_all_row, low_r, low_s, k))
    low_half = start(remote(low_all_row, low_all_row, lowsib.at[0], lowsib.at[1], sibling))
    hop_step(REACH - 1, sibs[REACH - 1])
    each(R, lambda k: row_recv(lowx, lowx_r, lowx_s, k))
    lows_all = lowx[...].reshape(T, 128)
    qup_g[...] = 2.0 * tn(lows_all, qg_all[...].reshape(T, H))[RANK:2 * RANK]
    low_half.wait_recv()
    lb = low_all[...].reshape(T, 128)
    oup_g[...] = 2.0 * tn(lb, w_all[...].reshape(T, D))[0:RANK]
    qdown_g[...] = 2.0 * tn(lb, n_all[...].reshape(T, D))[RANK:2 * RANK]
    low_back = low_all[z, core][:, RANK:2 * RANK]
    final = final + 2.0 * nn(low_back, qdown_t[...])
    for ch in (0, 1):
        for d in dirs:
            if length(d, ch) > 0:
                hops[d, ch, REACH - 1].wait_recv()
                final = final + hop_in[0 if d == 1 else 1, ch, REACH - 1].astype(F32)
    dots[row] = jnp.broadcast_to(
        jnp.sum(hf * gf * final, axis=1, keepdims=True), (B, 128))
    row_bcast(dots.at[row], dots, dot_s, dot_r)
    each(R, lambda k: row_recv(att_all, att_r, att_s, k))
    odown_g[...] = 2.0 * tn(lows_all, att_all[...].reshape(T, H))[0:RANK]
    inv = inv_own[:, 0:1]
    base = w_own.astype(F32) + inv * gf * final
    each(R, lambda k: row_recv(dots, dot_r, dot_s, k))
    dsum = dots[0]
    for i in range(1, R):
        dsum = dsum + dots[i]
    igrad[...] = base - hf * (inv * inv * inv * dsum[:, 0:1] * (1.0 / MODEL_WIDTH))

    for wait in drains:
        wait()


def per_device(
    hidden, cotangent, importance, positions, segments, norm_gain, query_weight_matrix,
    key_weight, value_weight_matrix, output_weight_matrix, query_down_factor, query_up_factor,
    output_down_factor, out_up,
):
    R = lax.axis_size("row")
    C = lax.axis_size("col")
    Z = C // 2
    B, D = hidden.shape
    H = query_weight_matrix.shape[1]
    S = 2 * B
    CH = Z // REACH
    vmem = pl.BlockSpec(memory_space=pltpu.VMEM)
    dma = pltpu.SemaphoreType.DMA
    outs = (
        jax.ShapeDtypeStruct((B, D), F32),
        jax.ShapeDtypeStruct((RANK, D), F32),
        jax.ShapeDtypeStruct((RANK, H), F32),
        jax.ShapeDtypeStruct((RANK, H), F32),
        jax.ShapeDtypeStruct((RANK, D), F32),
    )
    scratch = [
        pltpu.VMEM((Z, 2, B, D), BF16),
        pltpu.VMEM((Z, 2, B, D), BF16),
        pltpu.VMEM((Z, S, D), BF16),
        pltpu.VMEM((Z, 2, B, 128), BF16),
        pltpu.VMEM((2, GROUP, HEAD // GROUP, D), BF16),
        pltpu.VMEM((R, B, 128), F32),
        pltpu.VMEM((R, S, H), BF16),
        pltpu.VMEM((R, S, H), BF16),
        pltpu.VMEM((R, S, 3 * HEAD), BF16),
        pltpu.VMEM((R, S, 3 * HEAD), BF16),
        pltpu.VMEM((R, S, H), BF16),
        pltpu.VMEM((R, S, H), BF16),
        pltpu.VMEM((R, S, 2 * HEAD), BF16),
        pltpu.VMEM((R, S, 128), BF16),
        pltpu.VMEM((R, S, 2 * HEAD), BF16),
        pltpu.VMEM((R, S, 2 * HEAD), BF16),
        pltpu.VMEM((R, S, H), BF16),
        pltpu.VMEM((R, S, 2 * HEAD), BF16),
        pltpu.VMEM((R, S, H), BF16),
        pltpu.VMEM((R, B, 128), F32),
        pltpu.VMEM((3, B, 128), F32),
        pltpu.VMEM((Z, B, 128), F32),
        pltpu.VMEM((R, 2, B, 128), BF16),
        pltpu.VMEM((REACH, CH * S, D), F32),
        pltpu.VMEM((REACH, CH, B, D), F32),
        pltpu.VMEM((REACH, CH, B, D), BF16),
        pltpu.VMEM((REACH, CH, B, D), BF16),
        pltpu.VMEM((2, 2, REACH, B, D), BF16),
        pltpu.VMEM((2, 2, REACH, B, D), BF16),
        dma((2, 2, 2, REACH)), dma((2, 2, 2, REACH)),
        dma((2, REACH, 4)), dma((2, REACH, 4)),
        dma((R,)), dma((R,)),
        dma((Z,)), dma((Z,)), dma((2,)),
        dma((3, 2)), dma((3, 2)),
        dma((R,)), dma((R,)),
        dma((R,)), dma((R,)),
        dma((R,)), dma((R,)),
        dma((R,)), dma((R,)),
        dma((R,)), dma((R,)),
        dma((R,)), dma((R,)),
        dma((R,)), dma((R,)),
        dma((R,)), dma((R,)),
        dma((R,)), dma((R,)),
        dma((2,)), dma((Z,)), dma((Z,)),
        dma((R,)), dma((R,)), dma((2,)),
        dma((REACH,)), dma((REACH,)),
        dma((2, 2, REACH)), dma((2, 2, REACH)),
        dma((R,)), dma((R,)),
    ]
    input_grad, qdown_g, qup_g, odown_g, oup_g = pl.pallas_call(
        functools.partial(kernel, R, Z),
        out_shape=outs,
        in_specs=[vmem] * 14,
        out_specs=[vmem] * 5,
        scratch_shapes=scratch,
        compiler_params=pltpu.CompilerParams(
            collective_id=0, has_side_effects=True, vmem_limit_bytes=56 * 1024 * 1024),
        name="attention_backward",
    )(
        hidden, cotangent, importance, positions, segments, norm_gain, query_weight_matrix,
        query_down_factor.T, key_weight.T, value_weight_matrix.T, output_weight_matrix, out_up,
        output_down_factor.T, query_up_factor,
    )
    return input_grad, qdown_g.T, qup_g, odown_g.T, oup_g


def solution(mesh):
    placed = (
        P("col", "row"), P("col", "row"), P("col"), P("col"), P("col"), P("row"),
        P("row", "col"), P("row", "col"), P("row", "col"), P("col", "row"),
        P("row", None), P(None, "col"), P("col", None), P(None, "row"),
    )
    return jax.shard_map(
        per_device,
        mesh=mesh,
        in_specs=placed,
        out_specs=(P("col", "row"), P("row", None), P(None, "col"), P("col", None), P(None, "row")),
        check_vma=False,
    )
```

time: 149 us -> 127 us (0.85)
  Pallas kernels: 136 us -> 121 us
  local copies, waits for them, and re-layouts: 8.69 us -> 5.21 us
  other arithmetic: 2.93 us -> 0 us
    pallas_call x1, Pallas kernels: 136 us -> 121 us  [per_device(): pl.pallas_call(functools.partial(kernel, R, Z), out_shape=outs, in_specs=...]
    pallas_call x2 -> x0, local copies, waits for them, and re-layouts: 3.69 us -> none  [per_device(): pl.pallas_call(functools.partial(kernel, R, Z), out_shape=outs, in_specs=...]
    transpose x1 -> x0, other arithmetic: 1.57 us -> none  [per_device(): kvt = jnp.concatenate([key_weight, value_weight_matrix], axis=1).T]
    unnamed x21 -> x11, local copies, waits for them, and re-layouts: 4.41 us -> 5.21 us
where the time goes in v2:
time: 127 us
  Pallas kernels  121 us (95%)
  local copies, waits for them, and re-layouts  5.21 us (4%)
    pallas_call x1, Pallas kernels, per_device(): pl.pallas_call(functools.partial(kernel, R, Z), out_shape=outs, in_specs=...  121 us
    unnamed x11, local copies, waits for them, and re-layouts  5.21 us

profile of v2, /device:TPU:1, one launch (start us, length us, event | category | flops | bytes accessed | tf_op | source)
XLA Modules:
  0.0 126.9 jit_solution(18015014928175305496)
XLA Ops:
  0.6 121.0 %attention_backward.1 = (f32[16,1024]{1,0:T(8,128)}, f32[64,1024]{1,0:T(8,128)}, f32[64,512]{1,0:T(8,128)}, f32[64,512]{1,0:T(8,128)}, f32[64,1024]{1,0:T(8,128)}) custom-call(bf16[16,1024]{1,0:T(8,128)(2,1)} %hid.1, bf16[16,1024]{1,0:T(8,128)(2,1)} %cot.1, bf16[16]{0:T(256)(128)(2,1)} %imp.1, s32[16]{0:T(128)} %posn.1, s32[16]{0:T(128)} %segm.1, ...), custom_call_target="tpu_custom_call" | custom-call | tf_op jit(solution)/shard_map/attention_backward/pallas_call | solution.py:544
  121.7 1.5 %copy.24 = f32[16,1024]{1,0:T(8,128)} copy(f32[16,1024]{1,0:T(8,128)} %get-tuple-element.20) | data formatting | bytes 131072
  123.2 0.0 copy-start.2
  123.2 0.0 copy-start.1
  123.2 1.7 %copy.25 = f32[1024,64]{0,1:T(8,128)} copy(f32[1024,64]{0,1:T(8,128)} %bitcast.6) | data formatting | bytes 524288
  124.9 0.0 copy-done.2
  124.9 0.0 copy-start
  124.9 0.7 copy.26
  125.5 0.0 copy-done.1
  125.5 0.7 copy.27
  126.2 0.0 copy-done
  126.2 0.7 copy.28
Async XLA Ops:
  123.2 1.7 %copy-start.2 = (f32[64,512]{1,0:T(8,128)S(1)}, f32[64,512]{1,0:T(8,128)}, u32[]{:S(2)}) copy-start(f32[64,512]{1,0:T(8,128)} %get-tuple-element.22) | copy-start | bytes 393220
  123.2 2.4 %copy-start.1 = (f32[64,512]{1,0:T(8,128)S(1)}, f32[64,512]{1,0:T(8,128)}, u32[]{:S(2)}) copy-start(f32[64,512]{1,0:T(8,128)} %get-tuple-element.13) | copy-start | bytes 393220
  124.9 1.3 %copy-start = (f32[64,1024]{1,0:T(8,128)S(1)}, f32[64,1024]{1,0:T(8,128)}, u32[]{:S(2)}) copy-start(f32[64,1024]{1,0:T(8,128)} %get-tuple-element.24) | copy-start | bytes 786436

commit v3 on v2

--- a/solution.py
+++ b/solution.py
@@ -21,6 +21,8 @@
 F32 = jnp.float32
 BF16 = jnp.bfloat16
 REACH = 4
+NEAR = 3
+STEPS = 4
 
 
 def nn(a, b):
@@ -44,14 +46,16 @@
 
 def kernel(
     R, Z,
-    hid, cot, imp, posn, segm, gain, wq, qdown_t, kw_t, vw_t, wo, oup, odown_t, qup,
+    hid, cot, imp, posn, segm, gain,
+    wq_hbm, qdown_hbm, kw_hbm, vw_hbm, wo_hbm, oup_hbm, odown_hbm, qup_hbm,
     igrad, qdown_g, qup_g, odown_g, oup_g,
+    wq, wo, oup, odown_t, qup, small,
     h_all, w_all, n_all, aux_all, kvt,
-    ssq, part_w, rx_w, part_kv, rx_kv, part_q, rx_q, kvx, lowx, kvpart, kvrx,
+    ssq, part_w, rx_w, part_kv, rx_kv, part_q, rx_q, kvgrp, kvx, lowx, kvpart, kvrx,
     qg_all, kvg_all, att_all, dots,
     lown, lowz, low_all, gq, own, sib_out, sib_in, hop_out, hop_in,
-    ring_s, ring_r, sib_s, sib_r, ssq_s, ssq_r, aux_s, aux_r, auxsib, kvt_s, kvt_r,
-    rsw_s, rsw_r, rsk_s, rsk_r, rsq_s, rsq_r, kvx_s, kvx_r, lowx_s, lowx_r,
+    load, ring_s, ring_r, sib_s, sib_r, ssq_s, ssq_r, aux_s, aux_r, auxsib, kvt_s, kvt_r,
+    rsw_s, rsw_r, rsk_s, rsk_r, rsq_s, rsq_r, grp_s, grp_r, kvx_s, kvx_r, lowx_s, lowx_r,
     kvp_s, kvp_r, qg_s, qg_r, kvg_s, kvg_r, att_s, att_r,
     lowp, lowz_s, lowz_r, low_s, low_r, lowsib, sg_s, sg_r, hop_s, hop_r, dot_s, dot_r,
 ):
@@ -62,7 +66,7 @@
     B, D = hid.shape
     S = 2 * B
     T = S * Z
-    H = wo.shape[0]
+    H = wo_hbm.shape[0]
     heads = H // HEAD
     counts = {1: Z // 2, -1: Z - 1 - Z // 2}
     dirs = (1, -1)
@@ -115,6 +119,25 @@
             s = zmod(z + k)
             remote(dst_of(s), dst_of(s), ss.at[k], rs.at[s], at_z(z + k)).wait_recv()
         each(Z, one)
+
+    loads = {}
+    for i, (name, src, dst) in enumerate((
+        ("oup", oup_hbm, oup), ("kw", kw_hbm, small.at[0]), ("vw", vw_hbm, small.at[1]),
+        ("qd0", qdown_hbm.at[pl.ds(0, 32)], small.at[2]),
+        ("qd1", qdown_hbm.at[pl.ds(32, 32)], small.at[3]),
+        ("wo", wo_hbm, wo), ("wq", wq_hbm, wq), ("odown", odown_hbm, odown_t),
+        ("qup", qup_hbm, qup),
+    )):
+        loads[name] = pltpu.make_async_copy(src, dst, load.at[i])
+
+    def loaded(*names):
+        for name in names:
+            loads[name].wait()
+
+    def flush():
+        for wait in drains:
+            wait()
+        drains.clear()
 
     barrier = pltpu.get_barrier_semaphore()
     each(R, lambda k: pl.semaphore_signal(
@@ -124,6 +147,8 @@
     pl.semaphore_signal(barrier, inc=1, device_id=sibling, device_id_type=MESH)
     pl.semaphore_signal(
         barrier, inc=1, device_id={"col": pair * 2 + 1 - core}, device_id_type=MESH)
+    for cp in loads.values():
+        cp.start()
 
     diagonal = (lax.broadcasted_iota(jnp.int32, (B, B), 0)
                 == lax.broadcasted_iota(jnp.int32, (B, B), 1))
@@ -137,21 +162,22 @@
              * column(jnp.minimum(imp[...].astype(F32), CAP))).astype(BF16)
     w_all[z, core] = w_own
     h_all[z, core] = hid[...]
-    ssq[row] = jnp.broadcast_to(jnp.sum(hf * hf, axis=1, keepdims=True), (B, 128))
+    loaded("oup")
+    ssq[row] = jnp.concatenate([
+        jnp.broadcast_to(jnp.sum(hf * hf, axis=1, keepdims=True), (B, 128 - RANK)),
+        nt(w_own, oup[...])], axis=1)
     member = lax.rem(col, GROUP)
-    kvt[0, member] = kw_t[...]
-    kvt[1, member] = vw_t[...]
     pl.semaphore_wait(barrier, R - 1 + Z - 1 + 2)
 
-    arrays = (w_all, h_all)
+    arrays = (h_all, w_all)
 
     def length(d, ch):
-        return min(REACH, counts[d]) if ch == 0 else max(counts[d] - REACH, 0)
+        return NEAR if ch == 0 else counts[d] - NEAR
 
     def ring_send(a, d, ch, t):
-        off = t if ch == 0 else (0 if t == 0 else REACH + t)
+        off = t if ch == 0 else (0 if t == 0 else NEAR + t)
         block = arrays[a].at[zmod(z - d * off), core]
-        target = z + d * (REACH + 1 if ch == 1 and t == 0 else 1)
+        target = z + d * (NEAR + 1 if ch == 1 and t == 0 else 1)
         i = 0 if d == 1 else 1
         return start(remote(
             block, block, ring_s.at[a, i, ch, t], ring_r.at[a, i, ch, t], at_z(target)))
@@ -161,7 +187,7 @@
     def sib_send(a, t, i, off):
         block = arrays[a].at[zmod(z + off), core]
         cp = start(remote(block, block, sib_s.at[a, t, i], sib_r.at[a, t, i], sibling))
-        halves.setdefault((a, t), []).append(cp)
+        halves.setdefault((a, min(t, STEPS - 1)), []).append(cp)
 
     flying = {}
     for a in range(2):
@@ -171,9 +197,10 @@
                     flying[a, d, ch] = ring_send(a, d, ch, 0)
     row_bcast(ssq.at[row], ssq, ssq_s, ssq_r)
     for a in range(2):
-        sib_send(a, REACH - 1, 3, 0)
+        sib_send(a, STEPS, 3, 0)
 
     def ring_step(t):
+        came = []
         for a in range(2):
             i = 0
             for ch in (1, 0):
@@ -183,35 +210,32 @@
                     flying[a, d, ch].wait_recv()
                     if t + 1 < length(d, ch):
                         flying[a, d, ch] = ring_send(a, d, ch, t + 1)
-                    sib_send(a, t, i, -d * (t + 1 + (REACH if ch else 0)))
+                    came.append((a, t, i, -d * (t + 1 + (NEAR if ch else 0))))
                     i += 1
+        for arrival in came:
+            sib_send(*arrival)
 
     def chips_of(t):
-        found = [-d * (t + 1 + (REACH if ch else 0))
-                 for ch in (1, 0) for d in dirs if t < length(d, ch)]
-        return found + [0] if t == REACH - 1 else found
-
-    groups = [chips_of(t) for t in range(REACH)]
-
-    kvt_cp = []
-    for i, dev in enumerate((sibling, {"col": pair * 2 + core}, {"col": pair * 2 + 1 - core})):
-        for half in range(2):
-            kvt_cp.append(start(remote(
-                kvt.at[half, member], kvt.at[half, member], kvt_s.at[i, half],
-                kvt_r.at[i, half], dev)))
+        return [-d * (t + 1 + (NEAR if ch else 0))
+                for ch in (1, 0) for d in dirs if t < length(d, ch)]
+
+    groups = [chips_of(t) for t in range(STEPS - 1)]
+    groups.append(chips_of(STEPS - 1) + chips_of(STEPS) + [0])
+
     ring_step(0)
     each(R, lambda k: row_recv(ssq, ssq_r, ssq_s, k))
     total = ssq[0]
     for i in range(1, R):
         total = total + ssq[i]
-    inv_own = lax.rsqrt(total * (1.0 / MODEL_WIDTH) + EPS)
+    inv_own = lax.rsqrt(total[:, 0:1] * (1.0 / MODEL_WIDTH) + EPS)
     lane = lax.broadcasted_iota(jnp.int32, (B, 128), 1)
     hi = inv_own.astype(BF16).astype(F32)
     mid = (inv_own - hi).astype(BF16).astype(F32)
     lo = inv_own - hi - mid
     p_own = posn[...]
     p_hi = lax.div(p_own, 64)
-    tile = jnp.where(lane == 0, hi, jnp.where(lane == 1, mid, lo))
+    tile = jnp.where(lane >= 128 - RANK, total, jnp.where(lane == 0, hi, jnp.where(
+        lane == 1, mid, lo)))
     for i, v in ((3, p_hi), (4, p_own - p_hi * 64), (5, segm[...])):
         tile = jnp.where(lane == i, column(v.astype(F32)), tile)
     aux_all[z, core] = tile.astype(BF16)
@@ -246,23 +270,20 @@
 
     def project_w(t):
         g = groups[t]
-        for cp in halves[0, t]:
+        for cp in halves[1, t]:
             cp.wait_recv()
         store(part_w, g, nt(rows_of(w_all, g, D), wo[...]).astype(BF16))
         rs_send(g, part_w, rx_w, rsw_s, rsw_r)
 
     def project_kv(t):
         g = groups[t]
-        for cp in halves[1, t]:
+        for cp in halves[0, t]:
             cp.wait_recv()
         ax = rows_of(aux_all, g, 128).astype(F32)
         h = rows_of(h_all, g, D).astype(F32)
         n = (h * (ax[:, 0:1] + ax[:, 1:2] + ax[:, 2:3]) * gf).astype(BF16)
         store(n_all, g, n)
-        store(part_kv, g, nt(n, kvt[...].reshape(2 * HEAD, D)).astype(BF16), slice(0, 2 * HEAD))
-        store(part_kv, g, jnp.concatenate(
-            [nt(rows_of(w_all, g, D), oup[...]), nt(n, qdown_t[...])], axis=1).astype(BF16),
-            slice(2 * HEAD, 3 * HEAD))
+        store(part_kv, g, nt(n, small[...].reshape(128, D)).astype(BF16))
         rs_send(g, part_kv, rx_kv, rsk_s, rsk_r)
 
     def project_q(t):
@@ -271,23 +292,32 @@
         rs_send(g, part_q, rx_q, rsq_s, rsq_r)
 
     ring_step(1)
+    loaded("wo")
     project_w(0)
     ring_step(2)
-    project_w(1)
     z_recv(lambda s: aux_all.at[s, core], aux_s, aux_r)
     aux_half = start(remote(
         aux_all.at[:, core], aux_all.at[:, core], auxsib.at[0], auxsib.at[1], sibling))
+    project_w(1)
+    loaded("kw", "vw", "qd0", "qd1", "wq")
+    aux_half.wait_recv()
+    project_kv(0)
+    project_q(0)
     ring_step(3)
+    project_kv(1)
+    project_q(1)
     project_w(2)
-    aux_half.wait_recv()
-    for cp in kvt_cp:
-        cp.wait_recv()
-    for t in range(3):
-        project_kv(t)
+    ring_step(4)
+    project_kv(2)
+    project_kv(3)
+    project_q(2)
+    project_q(3)
     project_w(3)
-    project_kv(3)
-    for t in range(4):
-        project_q(t)
+    kvt[:, member] = small[0:2]
+    kvt_own = kvt.at[:, member]
+    kvt_sib = start(remote(kvt_own, kvt_own, kvt_s.at[0], kvt_r.at[0], sibling))
+    kvt_pair = start(remote(
+        kvt_own, kvt_own, kvt_s.at[1], kvt_r.at[1], {"col": pair * 2 + core}))
     rs_drain(part_w, rx_w, rsw_s, rsw_r)
     rs_drain(part_kv, rx_kv, rsk_s, rsk_r)
     rs_drain(part_q, rx_q, rsq_s, rsq_r)
@@ -322,17 +352,26 @@
             acc = acc + rx[peer(k)].astype(F32)
         return acc
 
-    dA = rs_sum(part_w, rx_w, rsw_s, rsw_r)
     kvl = rs_sum(part_kv, rx_kv, rsk_s, rsk_r)
-    kvx[row, :, 0:HEAD] = rotate(kvl[:, 0:HEAD]).astype(BF16)
-    kvx[row, :, HEAD:2 * HEAD] = kvl[:, HEAD:2 * HEAD].astype(BF16)
+    kvgrp[member] = kvl
+    kvl_cp = []
+    for i, dev in enumerate((sibling, {"col": pair * 2 + core}, {"col": pair * 2 + 1 - core})):
+        kvl_cp.append(start(remote(
+            kvgrp.at[member], kvgrp.at[member], grp_s.at[i], grp_r.at[i], dev)))
+    low = kvl.astype(BF16)
+    lowx[row] = low
+    loaded("qup", "odown")
+    ql = 2.0 * nn(low[:, RANK:2 * RANK], qup[...])
+    dA = 2.0 * nn(aux_all[row].reshape(S, 128)[:, 128 - RANK:128], odown_t[...])
+    for cp in kvl_cp:
+        cp.wait_recv()
+    part = HEAD // GROUP
+    kl, vl = (jnp.concatenate(
+        [kvgrp[g][:, half * part:(half + 1) * part] for g in range(GROUP)], axis=1)
+        for half in range(2))
+    kvx[row, :, 0:HEAD] = rotate(kl).astype(BF16)
+    kvx[row, :, HEAD:2 * HEAD] = vl.astype(BF16)
     row_bcast(kvx.at[row], kvx, kvx_s, kvx_r)
-    low = kvl[:, 2 * HEAD:3 * HEAD].astype(BF16)
-    lowx[row] = low
-    row_bcast(lowx.at[row], lowx, lowx_s, lowx_r)
-    dA = (dA + 2.0 * nn(low[:, 0:RANK], odown_t[...])).astype(BF16)
-    grads = jnp.concatenate([dA[:, i * HEAD:(i + 1) * HEAD] for i in range(heads)], axis=0)
-    ql = 2.0 * nn(low[:, RANK:2 * RANK], qup[...])
     ql = ql + rs_sum(part_q, rx_q, rsq_s, rsq_r)
     queries = jnp.concatenate(
         [rotate(ql[:, i * HEAD:(i + 1) * HEAD]).astype(BF16) for i in range(heads)], axis=0)
@@ -344,6 +383,8 @@
     shifted = jnp.exp(scores - jnp.max(scores, axis=1, keepdims=True))
     probs = shifted / jnp.sum(shifted, axis=1, keepdims=True)
     narrow = probs.astype(BF16)
+    dA = (dA + rs_sum(part_w, rx_w, rsw_s, rsw_r)).astype(BF16)
+    grads = jnp.concatenate([dA[:, i * HEAD:(i + 1) * HEAD] for i in range(heads)], axis=0)
     pgrad = nt(grads, values)
     rdot = jnp.sum(probs * pgrad, axis=1, keepdims=True)
     sgrad = (probs * (pgrad - rdot) * SCALE).astype(BF16)
@@ -369,6 +410,9 @@
     lown[0] = jnp.where(core == 0, inner[0:B], inner[B:S])
     lown[1] = jnp.where(core == 0, inner[B:S], inner[0:B])
     low_pair = start(remote(lown.at[1], lown.at[2], lowp.at[0], lowp.at[1], sibling))
+    kvt_pair.wait_recv()
+    other = kvt.at[:, 2 * lax.rem(pair, 2) + core]
+    kvt_other = start(remote(other, other, kvt_s.at[2], kvt_r.at[2], sibling))
     kacc = rs_sum(kvpart, kvrx, kvp_s, kvp_r)
     kvg_all[row, :, 0:HEAD] = unrotate(kacc[:, 0:HEAD]).astype(BF16)
     kvg_all[row, :, HEAD:2 * HEAD] = kacc[:, HEAD:2 * HEAD].astype(BF16)
@@ -376,12 +420,20 @@
     low_pair.wait_recv()
     lowz[z] = lown[0] + lown[2]
     z_bcast(lowz.at[z], lambda s: lowz.at[s], lowz_s, lowz_r)
+    row_bcast(lowx.at[row], lowx, lowx_s, lowx_r)
     row_bcast(att_all.at[row], att_all, att_s, att_r)
 
     each(R, lambda k: row_recv(qg_all, qg_r, qg_s, k))
     order = list(reversed(range(REACH)))
+
+    def hop_length(d, ch):
+        return REACH if ch == 0 else counts[d] - REACH
+
+    bgroups = [[-d * (t + 1 + (REACH if ch else 0))
+                for ch in (1, 0) for d in dirs if t < hop_length(d, ch)] for t in range(REACH)]
+    bgroups[REACH - 1].append(0)
     for t in order:
-        gq[t, 0:len(groups[t]) * S] = nt(rows_of(qg_all, groups[t], H), wq[...])
+        gq[t, 0:len(bgroups[t]) * S] = nt(rows_of(qg_all, bgroups[t], H), wq[...])
     z_recv(lambda s: lowz.at[s], lowz_s, lowz_r)
     inner = lowz[0]
     for i in range(1, Z):
@@ -389,9 +441,11 @@
     low_all[row, core] = inner.astype(BF16)
     row_bcast(low_all.at[row, core], low_all.at[:, core], low_s, low_r)
     each(R, lambda k: row_recv(kvg_all, kvg_r, kvg_s, k))
+    kvt_sib.wait_recv()
+    kvt_other.wait_recv()
 
     def backward(t):
-        g = groups[t]
+        g = bgroups[t]
         value = gq[t, 0:len(g) * S] + nn(
             rows_of(kvg_all, g, 2 * HEAD), kvt[...].reshape(2 * HEAD, D))
         value = value.reshape(len(g), 2, B, D)
@@ -420,7 +474,7 @@
                 if delta > last:
                     continue
                 i = 0 if d == 1 else 1
-                slot = groups[u].index(d * delta if d * delta in groups[u] else -d * delta)
+                slot = bgroups[u].index(d * delta if d * delta in bgroups[u] else -d * delta)
                 term = own[u, slot] + sib_in[u, slot].astype(F32)
                 if delta < last:
                     hops[d, ch, t - 1].wait_recv()
@@ -433,7 +487,7 @@
         sibs[t] = backward(u)
         if t > 0:
             hop_step(t - 1, sibs[t - 1])
-    own_slot = groups[REACH - 1].index(0)
+    own_slot = bgroups[REACH - 1].index(0)
     final = own[REACH - 1, own_slot] + sib_in[REACH - 1, own_slot].astype(F32)
     low_all_row = low_all.at[:, core]
     each(R, lambda k: row_recv(low_all_row, low_r, low_s, k))
@@ -442,23 +496,25 @@
     each(R, lambda k: row_recv(lowx, lowx_r, lowx_s, k))
     lows_all = lowx[...].reshape(T, 128)
     qup_g[...] = 2.0 * tn(lows_all, qg_all[...].reshape(T, H))[RANK:2 * RANK]
+    flush()
     low_half.wait_recv()
     lb = low_all[...].reshape(T, 128)
     oup_g[...] = 2.0 * tn(lb, w_all[...].reshape(T, D))[0:RANK]
     qdown_g[...] = 2.0 * tn(lb, n_all[...].reshape(T, D))[RANK:2 * RANK]
     low_back = low_all[z, core][:, RANK:2 * RANK]
-    final = final + 2.0 * nn(low_back, qdown_t[...])
+    final = final + 2.0 * nn(low_back, small[2:4].reshape(RANK, D))
     for ch in (0, 1):
         for d in dirs:
-            if length(d, ch) > 0:
+            if hop_length(d, ch) > 0:
                 hops[d, ch, REACH - 1].wait_recv()
                 final = final + hop_in[0 if d == 1 else 1, ch, REACH - 1].astype(F32)
     dots[row] = jnp.broadcast_to(
         jnp.sum(hf * gf * final, axis=1, keepdims=True), (B, 128))
     row_bcast(dots.at[row], dots, dot_s, dot_r)
     each(R, lambda k: row_recv(att_all, att_r, att_s, k))
-    odown_g[...] = 2.0 * tn(lows_all, att_all[...].reshape(T, H))[0:RANK]
-    inv = inv_own[:, 0:1]
+    odown_g[...] = 2.0 * tn(aux_all[...].reshape(T, 128), att_all[...].reshape(T, H))[128 - RANK:128]
+    inv = inv_own
+    flush()
     base = w_own.astype(F32) + inv * gf * final
     each(R, lambda k: row_recv(dots, dot_r, dot_s, k))
     dsum = dots[0]
@@ -466,8 +522,13 @@
         dsum = dsum + dots[i]
     igrad[...] = base - hf * (inv * inv * inv * dsum[:, 0:1] * (1.0 / MODEL_WIDTH))
 
-    for wait in drains:
-        wait()
+    flush()
+
+
+def finish(*refs):
+    n = len(refs) // 2
+    for i in range(n):
+        refs[n + i][...] = refs[i][...]
 
 
 def per_device(
@@ -492,6 +553,12 @@
         jax.ShapeDtypeStruct((RANK, D), F32),
     )
     scratch = [
+        pltpu.VMEM((D, H), BF16),
+        pltpu.VMEM((H, D), BF16),
+        pltpu.VMEM((RANK, D), BF16),
+        pltpu.VMEM((RANK, H), BF16),
+        pltpu.VMEM((RANK, H), BF16),
+        pltpu.VMEM((4, 32, D), BF16),
         pltpu.VMEM((Z, 2, B, D), BF16),
         pltpu.VMEM((Z, 2, B, D), BF16),
         pltpu.VMEM((Z, S, D), BF16),
@@ -500,10 +567,11 @@
         pltpu.VMEM((R, B, 128), F32),
         pltpu.VMEM((R, S, H), BF16),
         pltpu.VMEM((R, S, H), BF16),
-        pltpu.VMEM((R, S, 3 * HEAD), BF16),
-        pltpu.VMEM((R, S, 3 * HEAD), BF16),
+        pltpu.VMEM((R, S, HEAD), BF16),
+        pltpu.VMEM((R, S, HEAD), BF16),
         pltpu.VMEM((R, S, H), BF16),
         pltpu.VMEM((R, S, H), BF16),
+        pltpu.VMEM((GROUP, S, HEAD), F32),
         pltpu.VMEM((R, S, 2 * HEAD), BF16),
         pltpu.VMEM((R, S, 128), BF16),
         pltpu.VMEM((R, S, 2 * HEAD), BF16),
@@ -521,14 +589,16 @@
         pltpu.VMEM((REACH, CH, B, D), BF16),
         pltpu.VMEM((2, 2, REACH, B, D), BF16),
         pltpu.VMEM((2, 2, REACH, B, D), BF16),
-        dma((2, 2, 2, REACH)), dma((2, 2, 2, REACH)),
-        dma((2, REACH, 4)), dma((2, REACH, 4)),
+        dma((9,)),
+        dma((2, 2, 2, 8)), dma((2, 2, 2, 8)),
+        dma((2, 8, 4)), dma((2, 8, 4)),
         dma((R,)), dma((R,)),
         dma((Z,)), dma((Z,)), dma((2,)),
-        dma((3, 2)), dma((3, 2)),
-        dma((R,)), dma((R,)),
-        dma((R,)), dma((R,)),
-        dma((R,)), dma((R,)),
+        dma((3,)), dma((3,)),
+        dma((R,)), dma((R,)),
+        dma((R,)), dma((R,)),
+        dma((R,)), dma((R,)),
+        dma((3,)), dma((3,)),
         dma((R,)), dma((R,)),
         dma((R,)), dma((R,)),
         dma((R,)), dma((R,)),
@@ -541,10 +611,10 @@
         dma((2, 2, REACH)), dma((2, 2, REACH)),
         dma((R,)), dma((R,)),
     ]
-    input_grad, qdown_g, qup_g, odown_g, oup_g = pl.pallas_call(
+    results = pl.pallas_call(
         functools.partial(kernel, R, Z),
         out_shape=outs,
-        in_specs=[vmem] * 14,
+        in_specs=[vmem] * 6 + [pl.BlockSpec(memory_space=pl.ANY)] * 8,
         out_specs=[vmem] * 5,
         scratch_shapes=scratch,
         compiler_params=pltpu.CompilerParams(
@@ -555,6 +625,13 @@
         query_down_factor.T, key_weight.T, value_weight_matrix.T, output_weight_matrix, out_up,
         output_down_factor.T, query_up_factor,
     )
+    input_grad, qdown_g, qup_g, odown_g, oup_g = pl.pallas_call(
+        finish,
+        out_shape=outs,
+        in_specs=[vmem] * 5,
+        out_specs=[vmem] * 5,
+        name="place_results",
+    )(*results)
     return input_grad, qdown_g.T, qup_g, odown_g.T, oup_g
 
 

time: 127 us -> 119 us (0.937)
  local copies, waits for them, and re-layouts: 5.21 us -> 0 us
  Pallas kernels: 121 us -> 118 us
    unnamed x11 -> x0, local copies, waits for them, and re-layouts: 5.21 us -> none
    pallas_call x1, Pallas kernels: 121 us -> 116 us  [per_device(): pl.pallas_call(functools.partial(kernel, R, Z), out_shape=outs, in_specs=...]
    pallas_call x0 -> x1, Pallas kernels: none -> 2.1 us  [per_device(): pl.pallas_call(finish, out_shape=outs, in_specs=[vmem] * 5, out_specs=[vm...]
where the time goes in v3:
time: 119 us
  Pallas kernels  118 us (99%)
    pallas_call x1, Pallas kernels, per_device(): pl.pallas_call(functools.partial(kernel, R, Z), out_shape=outs, in_specs=...  116 us

profile of v3, /device:TPU:1, one launch (start us, length us, event | category | flops | bytes accessed | tf_op | source)
XLA Modules:
  0.0 119.0 jit_solution(1870678709743159982)
XLA Ops:
  0.6 116.3 %attention_backward.1 = (f32[16,1024]{1,0:T(8,128)}, f32[64,1024]{1,0:T(8,128)}, f32[64,512]{1,0:T(8,128)}, f32[64,512]{1,0:T(8,128)}, f32[64,1024]{1,0:T(8,128)}) custom-call(bf16[16,1024]{1,0:T(8,128)(2,1)} %hid.1, bf16[16,1024]{1,0:T(8,128)(2,1)} %cot.1, bf16[16]{0:T(256)(128)(2,1)} %imp.1, s32[16]{0:T(128)} %posn.1, s32[16]{0:T(128)} %segm.1, ...), custom_call_target="tpu_custom_call" | custom-call | tf_op jit(solution)/shard_map/attention_backward/pallas_call | solution.py:614
  116.9 2.1 %place_results.1 = (f32[16,1024]{1,0:T(8,128)}, f32[64,1024]{1,0:T(8,128)}, f32[64,512]{1,0:T(8,128)}, f32[64,512]{1,0:T(8,128)}, f32[64,1024]{1,0:T(8,128)}) custom-call(f32[16,1024]{1,0:T(8,128)} %get-tuple-element.15.refs_0_, f32[64,1024]{1,0:T(8,128)} %get-tuple-element.16.refs_1_, f32[64,512]{1,0:T(8,128)} %get-tuple-element.17.refs_2_, ...), custom_call_target="tpu_custom_call" | custom-call | tf_op jit(solution)/shard_map/place_results/pallas_call | solution.py:628

commit v4 on v3

--- a/solution.py
+++ b/solution.py
@@ -21,8 +21,9 @@
 F32 = jnp.float32
 BF16 = jnp.bfloat16
 REACH = 4
-NEAR = 3
+NEAR = 4
 STEPS = 4
+SHIFT = 3
 
 
 def nn(a, b):
@@ -51,11 +52,11 @@
     igrad, qdown_g, qup_g, odown_g, oup_g,
     wq, wo, oup, odown_t, qup, small,
     h_all, w_all, n_all, aux_all, kvt,
-    ssq, part_w, rx_w, part_kv, rx_kv, part_q, rx_q, kvgrp, kvx, lowx, kvpart, kvrx,
+    ssq, part_w, rx_w, part_h, rx_h, aux_s, low_nat, kvgrp, kvx, lowx, kvpart, kvrx,
     qg_all, kvg_all, att_all, dots,
     lown, lowz, low_all, gq, own, sib_out, sib_in, hop_out, hop_in,
-    load, ring_s, ring_r, sib_s, sib_r, ssq_s, ssq_r, aux_s, aux_r, auxsib, kvt_s, kvt_r,
-    rsw_s, rsw_r, rsk_s, rsk_r, rsq_s, rsq_r, grp_s, grp_r, kvx_s, kvx_r, lowx_s, lowx_r,
+    load, ring_s, ring_r, sib_s, sib_r, ssq_s, ssq_r, auxz_s, auxz_r, auxsib, kvt_s, kvt_r,
+    rsw_s, rsw_r, rsh_s, rsh_r, grp_s, grp_r, kvx_s, kvx_r, lowx_s, lowx_r,
     kvp_s, kvp_r, qg_s, qg_r, kvg_s, kvg_r, att_s, att_r,
     lowp, lowz_s, lowz_r, low_s, low_r, lowsib, sg_s, sg_r, hop_s, hop_r, dot_s, dot_r,
 ):
@@ -85,40 +86,33 @@
         return lax.rem(row + k, R)
 
     def each(n, f):
-        def step(k, carry):
+        for k in range(1, n):
             f(k)
-            return carry
-        lax.fori_loop(1, n, step, 0)
 
     def start(cp):
         cp.start()
         drains.append(cp.wait_send)
         return cp
 
-    def row_copy(src, dst, ss, rs, k):
-        return remote(src, dst, ss.at[k], rs, {"row": peer(k)})
+    def every(ref, ss, rs, device):
+        most = ref.at[pl.ds(0, R - 1)]
+        return remote(most, most, ss.at[0], rs.at[0], device)
 
     def row_bcast(src, dst_all, ss, rs):
-        def one(k):
-            return row_copy(src, dst_all.at[row], ss, rs.at[row], k)
-        each(R, lambda k: one(k).start())
-        drains.append(lambda: each(R, lambda k: one(k).wait_send()))
-
-    def row_recv(dst_all, rs, ss, k):
-        s = peer(k)
-        row_copy(dst_all.at[s], dst_all.at[s], ss, rs.at[s], k).wait_recv()
-
-    def z_bcast(src, dst_of, ss, rs):
-        def one(k):
-            return remote(src, dst_of(z), ss.at[k], rs.at[z], at_z(z + k))
-        each(Z, lambda k: one(k).start())
-        drains.append(lambda: each(Z, lambda k: one(k).wait_send()))
-
-    def z_recv(dst_of, ss, rs):
-        def one(k):
-            s = zmod(z + k)
-            remote(dst_of(s), dst_of(s), ss.at[k], rs.at[s], at_z(z + k)).wait_recv()
-        each(Z, one)
+        each(R, lambda k: remote(
+            src, dst_all.at[row], ss.at[0], rs.at[0], {"row": peer(k)}).start())
+        drains.append(lambda: every(dst_all, ss, rs, {"row": peer(1)}).wait_send())
+
+    def row_recv(dst_all, rs, ss):
+        every(dst_all, ss, rs, {"row": peer(1)}).wait_recv()
+
+    def z_bcast(src, dst_all, ss, rs):
+        each(Z, lambda k: remote(
+            src, dst_all.at[z], ss.at[0], rs.at[0], at_z(z + k)).start())
+        drains.append(lambda: every(dst_all, ss, rs, at_z(z + 1)).wait_send())
+
+    def z_recv(dst_all, ss, rs):
+        every(dst_all, ss, rs, at_z(z + 1)).wait_recv()
 
     loads = {}
     for i, (name, src, dst) in enumerate((
@@ -222,8 +216,13 @@
     groups = [chips_of(t) for t in range(STEPS - 1)]
     groups.append(chips_of(STEPS - 1) + chips_of(STEPS) + [0])
 
+    def slice_of(o, b):
+        return zmod(z + o + SHIFT * b), b
+
+    slices = {(c, b): ((c + SHIFT * b) % Z, b) for c in range(Z) for b in range(2)}
+
     ring_step(0)
-    each(R, lambda k: row_recv(ssq, ssq_r, ssq_s, k))
+    row_recv(ssq, ssq_r, ssq_s)
     total = ssq[0]
     for i in range(1, R):
         total = total + ssq[i]
@@ -238,91 +237,83 @@
         lane == 1, mid, lo)))
     for i, v in ((3, p_hi), (4, p_own - p_hi * 64), (5, segm[...])):
         tile = jnp.where(lane == i, column(v.astype(F32)), tile)
+    tile = jnp.where(lane == 6, col.astype(F32), tile)
+    tile = jnp.where(
+        lane == 7, lax.broadcasted_iota(jnp.int32, (B, 128), 0).astype(F32), tile)
     aux_all[z, core] = tile.astype(BF16)
-    z_bcast(aux_all.at[z, core], lambda s: aux_all.at[s, core], aux_s, aux_r)
-
-    def rs_copy(src, dst, ss, rs, p):
-        return remote(src.at[p], dst.at[row], ss.at[p], rs.at[row], {"row": p})
-
-    def rs_send(group, src, dst, ss, rs):
-        n = len(group)
-        for m in range(n):
-            turn = lax.rem(row + m, n)
-            delta = group[0]
-            for i in range(1, n):
-                delta = jnp.where(turn == i, group[i], delta)
-            p = zmod(z + delta)
-
-            @pl.when(p != row)
-            def _():
-                rs_copy(src, dst, ss, rs, p).start()
-
-    def rs_drain(src, dst, ss, rs):
-        drains.append(lambda: each(R, lambda k: rs_copy(src, dst, ss, rs, peer(k)).wait_send()))
+    z_bcast(aux_all.at[z, core], aux_all.at[:, core], auxz_s, auxz_r)
+
+    def rs_send(gi, src, dst, ss, rs):
+        for b in range(2):
+            for o in groups[gi]:
+                p = zmod(z + o + SHIFT * b)
+
+                @pl.when(p != row)
+                def _():
+                    remote(src.at[p, b], dst.at[row, b], ss.at[0], rs.at[0], {"row": p}).start()
+
+    def rs_drain(src, ss, rs):
+        drains.append(lambda: every(src, ss, rs, {"row": peer(1)}).wait_send())
 
     def rows_of(ref, group, width):
         return jnp.concatenate(
             [ref[zmod(z + o)].reshape(S, width) for o in group], axis=0)
 
-    def store(ref, group, value, at=slice(None)):
+    def store(ref, group, value, at):
         for i, o in enumerate(group):
-            ref[zmod(z + o), :, at] = value[i * S:(i + 1) * S]
+            for b in range(2):
+                r, half = slice_of(o, b)
+                ref[r, half, :, at] = value[i * S + b * B:i * S + (b + 1) * B]
 
     def project_w(t):
         g = groups[t]
         for cp in halves[1, t]:
             cp.wait_recv()
-        store(part_w, g, nt(rows_of(w_all, g, D), wo[...]).astype(BF16))
-        rs_send(g, part_w, rx_w, rsw_s, rsw_r)
-
-    def project_kv(t):
+        store(part_w, g, nt(rows_of(w_all, g, D), wo[...]).astype(BF16), slice(0, H))
+        rs_send(t, part_w, rx_w, rsw_s, rsw_r)
+
+    def project_h(t):
         g = groups[t]
         for cp in halves[0, t]:
             cp.wait_recv()
         ax = rows_of(aux_all, g, 128).astype(F32)
         h = rows_of(h_all, g, D).astype(F32)
         n = (h * (ax[:, 0:1] + ax[:, 1:2] + ax[:, 2:3]) * gf).astype(BF16)
-        store(n_all, g, n)
-        store(part_kv, g, nt(n, small[...].reshape(128, D)).astype(BF16))
-        rs_send(g, part_kv, rx_kv, rsk_s, rsk_r)
-
-    def project_q(t):
-        g = groups[t]
-        store(part_q, g, nn(rows_of(n_all, g, D), wq[...]).astype(BF16))
-        rs_send(g, part_q, rx_q, rsq_s, rsq_r)
+        for i, o in enumerate(g):
+            n_all[zmod(z + o)] = n[i * S:(i + 1) * S]
+        store(part_h, g, nt(n, small[...].reshape(128, D)).astype(BF16), slice(H, H + 128))
+        store(part_h, g, nn(n, wq[...]).astype(BF16), slice(0, H))
+        rs_send(t, part_h, rx_h, rsh_s, rsh_r)
 
     ring_step(1)
     loaded("wo")
     project_w(0)
     ring_step(2)
-    z_recv(lambda s: aux_all.at[s, core], aux_s, aux_r)
+    z_recv(aux_all.at[:, core], auxz_s, auxz_r)
     aux_half = start(remote(
         aux_all.at[:, core], aux_all.at[:, core], auxsib.at[0], auxsib.at[1], sibling))
     project_w(1)
     loaded("kw", "vw", "qd0", "qd1", "wq")
     aux_half.wait_recv()
-    project_kv(0)
-    project_q(0)
+    project_h(0)
     ring_step(3)
-    project_kv(1)
-    project_q(1)
+    project_h(1)
     project_w(2)
     ring_step(4)
-    project_kv(2)
-    project_kv(3)
-    project_q(2)
-    project_q(3)
+    project_h(2)
+    project_h(3)
     project_w(3)
     kvt[:, member] = small[0:2]
     kvt_own = kvt.at[:, member]
     kvt_sib = start(remote(kvt_own, kvt_own, kvt_s.at[0], kvt_r.at[0], sibling))
     kvt_pair = start(remote(
         kvt_own, kvt_own, kvt_s.at[1], kvt_r.at[1], {"col": pair * 2 + core}))
-    rs_drain(part_w, rx_w, rsw_s, rsw_r)
-    rs_drain(part_kv, rx_kv, rsk_s, rsk_r)
-    rs_drain(part_q, rx_q, rsq_s, rsq_r)
-
-    ax = aux_all[row].reshape(S, 128).astype(F32)
+    rs_drain(part_w, rsw_s, rsw_r)
+    rs_drain(part_h, rsh_s, rsh_r)
+
+    for (o, b), (r, half) in slices.items():
+        aux_s[r, half] = aux_all[o, b]
+    ax = aux_s[row].reshape(S, 128).astype(F32)
     pos = ax[:, 3:4] * 64.0 + ax[:, 4:5]
     lane_s = lax.broadcasted_iota(jnp.int32, (S, HEAD), 1)
     half_lane = lax.rem(lane_s, HEAD // 2).astype(F32)
@@ -339,20 +330,24 @@
     def unrotate(x):
         return x * cosine - swap(x) * sine
 
-    pick = (lax.broadcasted_iota(jnp.int32, (8, 128), 1) == 5).astype(BF16)
-    seg_key = nt(pick, aux_all[...].reshape(T, 128))[0:1, :]
-    token = row * S + lax.broadcasted_iota(jnp.int32, (S, T), 0)
-    allowed = (ax[:, 5:6] == seg_key) & (lax.broadcasted_iota(jnp.int32, (S, T), 1) <= token)
+    pick_row = lax.broadcasted_iota(jnp.int32, (8, 128), 0)
+    pick_lane = lax.broadcasted_iota(jnp.int32, (8, 128), 1)
+    pick = jnp.where(pick_row == 0, (pick_lane == 5).astype(F32), jnp.where(
+        pick_row == 1, jnp.where(pick_lane == 6, float(B), (pick_lane == 7).astype(F32)), 0.0))
+    of_key = nt(pick.astype(BF16), aux_s[...].reshape(T, 128))
+    token = ax[:, 6:7] * float(B) + ax[:, 7:8]
+    allowed = (ax[:, 5:6] == of_key[0:1, :]) & (of_key[1:2, :] <= token)
     allowed = jnp.concatenate([allowed.astype(F32)] * heads, axis=0) > 0.5
 
-    def rs_sum(part, rx, ss, rs):
-        acc = part[row].astype(F32)
+    def rs_sum(part, rx, ss, rs, width):
+        row_recv(rx, rs, ss)
+        acc = part[row].reshape(S, width).astype(F32)
         for k in range(1, R):
-            row_recv(rx, rs, ss, k)
-            acc = acc + rx[peer(k)].astype(F32)
+            acc = acc + rx[peer(k)].reshape(S, width).astype(F32)
         return acc
 
-    kvl = rs_sum(part_kv, rx_kv, rsk_s, rsk_r)
+    summed = rs_sum(part_h, rx_h, rsh_s, rsh_r, H + 128)
+    kvl = summed[:, H:H + 128]
     kvgrp[member] = kvl
     kvl_cp = []
     for i, dev in enumerate((sibling, {"col": pair * 2 + core}, {"col": pair * 2 + 1 - core})):
@@ -362,7 +357,7 @@
     lowx[row] = low
     loaded("qup", "odown")
     ql = 2.0 * nn(low[:, RANK:2 * RANK], qup[...])
-    dA = 2.0 * nn(aux_all[row].reshape(S, 128)[:, 128 - RANK:128], odown_t[...])
+    dA = 2.0 * nn(aux_s[row].reshape(S, 128)[:, 128 - RANK:128], odown_t[...])
     for cp in kvl_cp:
         cp.wait_recv()
     part = HEAD // GROUP
@@ -372,10 +367,10 @@
     kvx[row, :, 0:HEAD] = rotate(kl).astype(BF16)
     kvx[row, :, HEAD:2 * HEAD] = vl.astype(BF16)
     row_bcast(kvx.at[row], kvx, kvx_s, kvx_r)
-    ql = ql + rs_sum(part_q, rx_q, rsq_s, rsq_r)
+    ql = ql + summed[:, 0:H]
     queries = jnp.concatenate(
         [rotate(ql[:, i * HEAD:(i + 1) * HEAD]).astype(BF16) for i in range(heads)], axis=0)
-    each(R, lambda k: row_recv(kvx, kvx_r, kvx_s, k))
+    row_recv(kvx, kvx_r, kvx_s)
 
     keys = kvx[:, :, 0:HEAD].reshape(T, HEAD)
     values = kvx[:, :, HEAD:2 * HEAD].reshape(T, HEAD)
@@ -383,7 +378,7 @@
     shifted = jnp.exp(scores - jnp.max(scores, axis=1, keepdims=True))
     probs = shifted / jnp.sum(shifted, axis=1, keepdims=True)
     narrow = probs.astype(BF16)
-    dA = (dA + rs_sum(part_w, rx_w, rsw_s, rsw_r)).astype(BF16)
+    dA = (dA + rs_sum(part_w, rx_w, rsw_s, rsw_r, H)).astype(BF16)
     grads = jnp.concatenate([dA[:, i * HEAD:(i + 1) * HEAD] for i in range(heads)], axis=0)
     pgrad = nt(grads, values)
     rdot = jnp.sum(probs * pgrad, axis=1, keepdims=True)
@@ -391,12 +386,9 @@
     kvpart[:, :, 0:HEAD] = tn(sgrad, queries).astype(BF16).reshape(R, S, HEAD)
     kvpart[:, :, HEAD:2 * HEAD] = tn(narrow, grads).astype(BF16).reshape(R, S, HEAD)
 
-    def kvp_copy(k):
-        return remote(kvpart.at[peer(k)], kvrx.at[row], kvp_s.at[k], kvp_r.at[row],
-                      {"row": peer(k)})
-
-    each(R, lambda k: kvp_copy(k).start())
-    drains.append(lambda: each(R, lambda k: kvp_copy(k).wait_send()))
+    each(R, lambda k: remote(
+        kvpart.at[peer(k)], kvrx.at[row], kvp_s.at[0], kvp_r.at[0], {"row": peer(k)}).start())
+    drains.append(lambda: every(kvpart, kvp_s, kvp_r, {"row": peer(1)}).wait_send())
     qg = nn(sgrad, keys)
     for i in range(heads):
         qg_all[row, :, i * HEAD:(i + 1) * HEAD] = unrotate(qg[i * S:(i + 1) * S]).astype(BF16)
@@ -413,17 +405,17 @@
     kvt_pair.wait_recv()
     other = kvt.at[:, 2 * lax.rem(pair, 2) + core]
     kvt_other = start(remote(other, other, kvt_s.at[2], kvt_r.at[2], sibling))
-    kacc = rs_sum(kvpart, kvrx, kvp_s, kvp_r)
+    kacc = rs_sum(kvpart, kvrx, kvp_s, kvp_r, 2 * HEAD)
     kvg_all[row, :, 0:HEAD] = unrotate(kacc[:, 0:HEAD]).astype(BF16)
     kvg_all[row, :, HEAD:2 * HEAD] = kacc[:, HEAD:2 * HEAD].astype(BF16)
     row_bcast(kvg_all.at[row], kvg_all, kvg_s, kvg_r)
     low_pair.wait_recv()
     lowz[z] = lown[0] + lown[2]
-    z_bcast(lowz.at[z], lambda s: lowz.at[s], lowz_s, lowz_r)
+    z_bcast(lowz.at[z], lowz, lowz_s, lowz_r)
     row_bcast(lowx.at[row], lowx, lowx_s, lowx_r)
     row_bcast(att_all.at[row], att_all, att_s, att_r)
 
-    each(R, lambda k: row_recv(qg_all, qg_r, qg_s, k))
+    row_recv(qg_all, qg_r, qg_s)
     order = list(reversed(range(REACH)))
 
     def hop_length(d, ch):
@@ -432,22 +424,31 @@
     bgroups = [[-d * (t + 1 + (REACH if ch else 0))
                 for ch in (1, 0) for d in dirs if t < hop_length(d, ch)] for t in range(REACH)]
     bgroups[REACH - 1].append(0)
+
+    def sliced(ref, group):
+        blocks = []
+        for o in group:
+            for b in range(2):
+                r, half = slice_of(o, b)
+                blocks.append(ref[r, half * B:(half + 1) * B, :])
+        return jnp.concatenate(blocks, axis=0)
+
     for t in order:
-        gq[t, 0:len(bgroups[t]) * S] = nt(rows_of(qg_all, bgroups[t], H), wq[...])
-    z_recv(lambda s: lowz.at[s], lowz_s, lowz_r)
+        gq[t, 0:len(bgroups[t]) * S] = nt(sliced(qg_all, bgroups[t]), wq[...])
+    z_recv(lowz, lowz_s, lowz_r)
     inner = lowz[0]
     for i in range(1, Z):
         inner = inner + lowz[i]
     low_all[row, core] = inner.astype(BF16)
     row_bcast(low_all.at[row, core], low_all.at[:, core], low_s, low_r)
-    each(R, lambda k: row_recv(kvg_all, kvg_r, kvg_s, k))
+    row_recv(kvg_all, kvg_r, kvg_s)
     kvt_sib.wait_recv()
     kvt_other.wait_recv()
 
     def backward(t):
         g = bgroups[t]
         value = gq[t, 0:len(g) * S] + nn(
-            rows_of(kvg_all, g, 2 * HEAD), kvt[...].reshape(2 * HEAD, D))
+            sliced(kvg_all, g), kvt[...].reshape(2 * HEAD, D))
         value = value.reshape(len(g), 2, B, D)
         mine = core == 0
         sib_out[t, 0:len(g)] = jnp.where(mine, value[:, 1], value[:, 0]).astype(BF16)
@@ -490,18 +491,20 @@
     own_slot = bgroups[REACH - 1].index(0)
     final = own[REACH - 1, own_slot] + sib_in[REACH - 1, own_slot].astype(F32)
     low_all_row = low_all.at[:, core]
-    each(R, lambda k: row_recv(low_all_row, low_r, low_s, k))
+    row_recv(low_all_row, low_r, low_s)
     low_half = start(remote(low_all_row, low_all_row, lowsib.at[0], lowsib.at[1], sibling))
     hop_step(REACH - 1, sibs[REACH - 1])
-    each(R, lambda k: row_recv(lowx, lowx_r, lowx_s, k))
+    row_recv(lowx, lowx_r, lowx_s)
     lows_all = lowx[...].reshape(T, 128)
     qup_g[...] = 2.0 * tn(lows_all, qg_all[...].reshape(T, H))[RANK:2 * RANK]
     flush()
     low_half.wait_recv()
-    lb = low_all[...].reshape(T, 128)
+    for (o, b), (r, half) in slices.items():
+        low_nat[o, b] = low_all[r, half]
+    lb = low_nat[...].reshape(T, 128)
     oup_g[...] = 2.0 * tn(lb, w_all[...].reshape(T, D))[0:RANK]
     qdown_g[...] = 2.0 * tn(lb, n_all[...].reshape(T, D))[RANK:2 * RANK]
-    low_back = low_all[z, core][:, RANK:2 * RANK]
+    low_back = low_nat[z, core][:, RANK:2 * RANK]
     final = final + 2.0 * nn(low_back, small[2:4].reshape(RANK, D))
     for ch in (0, 1):
         for d in dirs:
@@ -511,12 +514,12 @@
     dots[row] = jnp.broadcast_to(
         jnp.sum(hf * gf * final, axis=1, keepdims=True), (B, 128))
     row_bcast(dots.at[row], dots, dot_s, dot_r)
-    each(R, lambda k: row_recv(att_all, att_r, att_s, k))
-    odown_g[...] = 2.0 * tn(aux_all[...].reshape(T, 128), att_all[...].reshape(T, H))[128 - RANK:128]
+    row_recv(att_all, att_r, att_s)
+    odown_g[...] = 2.0 * tn(aux_s[...].reshape(T, 128), att_all[...].reshape(T, H))[128 - RANK:128]
     inv = inv_own
     flush()
     base = w_own.astype(F32) + inv * gf * final
-    each(R, lambda k: row_recv(dots, dot_r, dot_s, k))
+    row_recv(dots, dot_r, dot_s)
     dsum = dots[0]
     for i in range(1, R):
         dsum = dsum + dots[i]
@@ -565,12 +568,12 @@
         pltpu.VMEM((Z, 2, B, 128), BF16),
         pltpu.VMEM((2, GROUP, HEAD // GROUP, D), BF16),
         pltpu.VMEM((R, B, 128), F32),
-        pltpu.VMEM((R, S, H), BF16),
-        pltpu.VMEM((R, S, H), BF16),
-        pltpu.VMEM((R, S, HEAD), BF16),
-        pltpu.VMEM((R, S, HEAD), BF16),
-        pltpu.VMEM((R, S, H), BF16),
-        pltpu.VMEM((R, S, H), BF16),
+        pltpu.VMEM((R, 2, B, H), BF16),
+        pltpu.VMEM((R, 2, B, H), BF16),
+        pltpu.VMEM((R, 2, B, H + 128), BF16),
+        pltpu.VMEM((R, 2, B, H + 128), BF16),
+        pltpu.VMEM((R, 2, B, 128), BF16),
+        pltpu.VMEM((Z, 2, B, 128), BF16),
         pltpu.VMEM((GROUP, S, HEAD), F32),
         pltpu.VMEM((R, S, 2 * HEAD), BF16),
         pltpu.VMEM((R, S, 128), BF16),
@@ -592,24 +595,23 @@
         dma((9,)),
         dma((2, 2, 2, 8)), dma((2, 2, 2, 8)),
         dma((2, 8, 4)), dma((2, 8, 4)),
-        dma((R,)), dma((R,)),
-        dma((Z,)), dma((Z,)), dma((2,)),
+        dma((1,)), dma((1,)),
+        dma((1,)), dma((1,)), dma((2,)),
         dma((3,)), dma((3,)),
-        dma((R,)), dma((R,)),
-        dma((R,)), dma((R,)),
-        dma((R,)), dma((R,)),
+        dma((1,)), dma((1,)),
+        dma((1,)), dma((1,)),
         dma((3,)), dma((3,)),
-        dma((R,)), dma((R,)),
-        dma((R,)), dma((R,)),
-        dma((R,)), dma((R,)),
-        dma((R,)), dma((R,)),
-        dma((R,)), dma((R,)),
-        dma((R,)), dma((R,)),
-        dma((2,)), dma((Z,)), dma((Z,)),
-        dma((R,)), dma((R,)), dma((2,)),
+        dma((1,)), dma((1,)),
+        dma((1,)), dma((1,)),
+        dma((1,)), dma((1,)),
+        dma((1,)), dma((1,)),
+        dma((1,)), dma((1,)),
+        dma((1,)), dma((1,)),
+        dma((2,)), dma((1,)), dma((1,)),
+        dma((1,)), dma((1,)), dma((2,)),
         dma((REACH,)), dma((REACH,)),
         dma((2, 2, REACH)), dma((2, 2, REACH)),
-        dma((R,)), dma((R,)),
+        dma((1,)), dma((1,)),
     ]
     results = pl.pallas_call(
         functools.partial(kernel, R, Z),

time: 119 us -> 113 us (0.950)
  Pallas kernels: 118 us -> 111 us
    pallas_call x1, Pallas kernels: 116 us -> 109 us  [per_device(): pl.pallas_call(functools.partial(kernel, R, Z), out_shape=outs, in_specs=...]
where the time goes in v4:
time: 113 us; the launch traced here: 112 us
  Pallas kernels  111 us (98%)
    pallas_call x1, Pallas kernels, per_device(): pl.pallas_call(functools.partial(kernel, R, Z), out_shape=outs, in_specs=...  109 us

profile of v4, /device:TPU:1, one launch (start us, length us, event | category | flops | bytes accessed | tf_op | source)
XLA Modules:
  0.0 111.9 jit_solution(33442281786262626)
XLA Ops:
  0.6 109.1 %attention_backward.1 = (f32[16,1024]{1,0:T(8,128)}, f32[64,1024]{1,0:T(8,128)}, f32[64,512]{1,0:T(8,128)}, f32[64,512]{1,0:T(8,128)}, f32[64,1024]{1,0:T(8,128)}) custom-call(bf16[16,1024]{1,0:T(8,128)(2,1)} %hid.1, bf16[16,1024]{1,0:T(8,128)(2,1)} %cot.1, bf16[16]{0:T(256)(128)(2,1)} %imp.1, s32[16]{0:T(128)} %posn.1, s32[16]{0:T(128)} %segm.1, ...), custom_call_target="tpu_custom_call" | custom-call | tf_op jit(solution)/shard_map/attention_backward/pallas_call | solution.py:616
  109.8 2.1 %place_results.1 = (f32[16,1024]{1,0:T(8,128)}, f32[64,1024]{1,0:T(8,128)}, f32[64,512]{1,0:T(8,128)}, f32[64,512]{1,0:T(8,128)}, f32[64,1024]{1,0:T(8,128)}) custom-call(f32[16,1024]{1,0:T(8,128)} %get-tuple-element.15.refs_0_, f32[64,1024]{1,0:T(8,128)} %get-tuple-element.16.refs_1_, f32[64,512]{1,0:T(8,128)} %get-tuple-element.17.refs_2_, ...), custom_call_target="tpu_custom_call" | custom-call | tf_op jit(solution)/shard_map/place_results/pallas_call | solution.py:630

commit v5 on v4

--- a/solution.py
+++ b/solution.py
@@ -184,8 +184,8 @@
         halves.setdefault((a, min(t, STEPS - 1)), []).append(cp)
 
     flying = {}
-    for a in range(2):
-        for ch in (1, 0):
+    for ch in (0, 1):
+        for a in range(2):
             for d in dirs:
                 if length(d, ch) > 0:
                     flying[a, d, ch] = ring_send(a, d, ch, 0)
@@ -193,21 +193,22 @@
     for a in range(2):
         sib_send(a, STEPS, 3, 0)
 
-    def ring_step(t):
+    def ring_part(t, ch):
         came = []
         for a in range(2):
-            i = 0
-            for ch in (1, 0):
-                for d in dirs:
-                    if t >= length(d, ch):
-                        continue
-                    flying[a, d, ch].wait_recv()
-                    if t + 1 < length(d, ch):
-                        flying[a, d, ch] = ring_send(a, d, ch, t + 1)
-                    came.append((a, t, i, -d * (t + 1 + (NEAR if ch else 0))))
-                    i += 1
+            for i, d in enumerate(dirs):
+                if t >= length(d, ch):
+                    continue
+                flying[a, d, ch].wait_recv()
+                if t + 1 < length(d, ch):
+                    flying[a, d, ch] = ring_send(a, d, ch, t + 1)
+                came.append((a, t, 2 * ch + i, -d * (t + 1 + (NEAR if ch else 0))))
         for arrival in came:
             sib_send(*arrival)
+
+    def ring_step(t):
+        ring_part(t, 0)
+        ring_part(t, 1)
 
     def chips_of(t):
         return [-d * (t + 1 + (NEAR if ch else 0))
@@ -221,7 +222,7 @@
 
     slices = {(c, b): ((c + SHIFT * b) % Z, b) for c in range(Z) for b in range(2)}
 
-    ring_step(0)
+    ring_part(0, 0)
     row_recv(ssq, ssq_r, ssq_s)
     total = ssq[0]
     for i in range(1, R):
@@ -242,6 +243,7 @@
         lane == 7, lax.broadcasted_iota(jnp.int32, (B, 128), 0).astype(F32), tile)
     aux_all[z, core] = tile.astype(BF16)
     z_bcast(aux_all.at[z, core], aux_all.at[:, core], auxz_s, auxz_r)
+    ring_part(0, 1)
 
     def rs_send(gi, src, dst, ss, rs):
         for b in range(2):
@@ -392,7 +394,6 @@
     qg = nn(sgrad, keys)
     for i in range(heads):
         qg_all[row, :, i * HEAD:(i + 1) * HEAD] = unrotate(qg[i * S:(i + 1) * S]).astype(BF16)
-    row_bcast(qg_all.at[row], qg_all, qg_s, qg_r)
     att = nn(narrow, values).astype(BF16)
     for i in range(heads):
         att_all[row, :, i * HEAD:(i + 1) * HEAD] = att[i * S:(i + 1) * S]
@@ -409,11 +410,10 @@
     kvg_all[row, :, 0:HEAD] = unrotate(kacc[:, 0:HEAD]).astype(BF16)
     kvg_all[row, :, HEAD:2 * HEAD] = kacc[:, HEAD:2 * HEAD].astype(BF16)
     row_bcast(kvg_all.at[row], kvg_all, kvg_s, kvg_r)
+    row_bcast(qg_all.at[row], qg_all, qg_s, qg_r)
     low_pair.wait_recv()
     lowz[z] = lown[0] + lown[2]
     z_bcast(lowz.at[z], lowz, lowz_s, lowz_r)
-    row_bcast(lowx.at[row], lowx, lowx_s, lowx_r)
-    row_bcast(att_all.at[row], att_all, att_s, att_r)
 
     row_recv(qg_all, qg_r, qg_s)
     order = list(reversed(range(REACH)))
@@ -442,6 +442,8 @@
     low_all[row, core] = inner.astype(BF16)
     row_bcast(low_all.at[row, core], low_all.at[:, core], low_s, low_r)
     row_recv(kvg_all, kvg_r, kvg_s)
+    row_bcast(lowx.at[row], lowx, lowx_s, lowx_r)
+    row_bcast(att_all.at[row], att_all, att_s, att_r)
     kvt_sib.wait_recv()
     kvt_other.wait_recv()
 

time: 113 us -> 113 us (level)
  no operation moved by 1% of the time
where the time goes in v5:
time: 113 us; the launch traced here: 111 us
  Pallas kernels  111 us (98%)
    pallas_call x1, Pallas kernels, per_device(): pl.pallas_call(functools.partial(kernel, R, Z), out_shape=outs, in_specs=...  108 us

profile of v5, /device:TPU:1, one launch (start us, length us, event | category | flops | bytes accessed | tf_op | source)
XLA Modules:
  0.0 111.2 jit_solution(6884569277264087862)
XLA Ops:
  0.6 108.4 %attention_backward.1 = (f32[16,1024]{1,0:T(8,128)}, f32[64,1024]{1,0:T(8,128)}, f32[64,512]{1,0:T(8,128)}, f32[64,512]{1,0:T(8,128)}, f32[64,1024]{1,0:T(8,128)}) custom-call(bf16[16,1024]{1,0:T(8,128)(2,1)} %hid.1, bf16[16,1024]{1,0:T(8,128)(2,1)} %cot.1, bf16[16]{0:T(256)(128)(2,1)} %imp.1, s32[16]{0:T(128)} %posn.1, s32[16]{0:T(128)} %segm.1, ...), custom_call_target="tpu_custom_call" | custom-call | tf_op jit(solution)/shard_map/attention_backward/pallas_call | solution.py:618
  109.0 2.1 %place_results.1 = (f32[16,1024]{1,0:T(8,128)}, f32[64,1024]{1,0:T(8,128)}, f32[64,512]{1,0:T(8,128)}, f32[64,512]{1,0:T(8,128)}, f32[64,1024]{1,0:T(8,128)}) custom-call(f32[16,1024]{1,0:T(8,128)} %get-tuple-element.15.refs_0_, f32[64,1024]{1,0:T(8,128)} %get-tuple-element.16.refs_1_, f32[64,512]{1,0:T(8,128)} %get-tuple-element.17.refs_2_, ...), custom_call_target="tpu_custom_call" | custom-call | tf_op jit(solution)/shard_map/place_results/pallas_call | solution.py:632
